TPU v7x, 256 devices: a whole 4x4x8 slice. The times are simulated.
256 devices in a mesh: section: 32 (over y_hi, z, core), tp: 8 (over y_lo, x).
Axes of the slice: x: 4, y: 4 (y_hi: 2, y_lo: 2; y = y_hi * 2 + y_lo), z: 8, core: 2. Of those that a mesh axis runs over, the one named last changes fastest.
Arguments:
- query_key_value_weight: bfloat16 [32, 2048, 3, 2048], P('section', None, None, 'tp'), may hold values from -6 to 6
- output_weight: bfloat16 [32, 2048, 2048], P('section', 'tp'), may hold values from -0.125 to 0.125
- ascending_query_key_value_weight: bfloat16 [32, 2048, 3, 2048], P('section', None, None, 'tp'), may hold values from -6 to 6
- ascending_output_weight: bfloat16 [32, 2048, 2048], P('section', 'tp'), may hold values from -0.125 to 0.125
- descending_saved_input: bfloat16 [32, 3, 128, 2048], P('section', None, 'tp'), may hold values from -6 to 6
- ascending_saved_input: bfloat16 [32, 3, 128, 2048], P('section', None, 'tp'), may hold values from -6 to 6
- descending_transit_gradient: bfloat16 [32, 128, 2048], P('section', 'tp'), may hold values from -4 to 4
- ascending_transit_gradient: bfloat16 [32, 128, 2048], P('section', 'tp'), may hold values from -4 to 4
- descending_loss_gradient: bfloat16 [2, 128, 2048], P(None, 'tp'), may hold values from -4 to 4
- ascending_loss_gradient: bfloat16 [2, 128, 2048], P(None, 'tp'), may hold values from -4 to 4
Outputs:
- grad_qkv: bfloat16 [32, 2048, 3, 2048], P('section', None, None, 'tp')
- grad_out: bfloat16 [32, 2048, 2048], P('section', 'tp')
- final_down: bfloat16 [32, 128, 2048], P('section', 'tp')
- final_up: bfloat16 [32, 128, 2048], P('section', 'tp')
All inputs are finite; a program needn't handle non-finite values.
Results may differ from a plain program's by a relative error of at most 0.029.
Values may be sent and summed in bfloat16 or wider, within the bound.
No kernel may reach another device: no remote copies, remote signals or barrier semaphores. Data moves between devices by JAX's collectives and lax.ppermute only.
A program may use at most 128 MiB of HBM per device.

v0:
```python
import functools

import jax
import jax.numpy as jnp
from jax import lax
from jax.experimental import pallas as pl
from jax.experimental.pallas import tpu as pltpu
from jax.sharding import PartitionSpec as P

HEAD = 128
TICKS = 3
EPSILON = 1e-05
MIB = 1 << 20
VMEM = pl.BlockSpec(memory_space=pltpu.VMEM)


def dot_nn(left, right):
    return jnp.dot(left, right, preferred_element_type=jnp.float32)


def dot_nt(left, right):
    return lax.dot_general(left, right, (((1,), (1,)), ((), ())), preferred_element_type=jnp.float32)


def dot_tn(left, right):
    return lax.dot_general(left, right, (((0,), (0,)), ((), ())), preferred_element_type=jnp.float32)


def normalized(raw):
    centre = raw - jnp.mean(raw, axis=-1, keepdims=True)
    inverse = lax.rsqrt(jnp.mean(centre * centre, axis=-1, keepdims=True) + EPSILON)
    return centre * inverse, inverse


def local_call(body, out_shape, operands, flops, moved, limit=16 * MIB):
    return pl.pallas_call(
        body,
        out_shape=out_shape,
        in_specs=[VMEM] * len(operands),
        out_specs=jax.tree.map(lambda _: VMEM, out_shape),
        compiler_params=pltpu.CompilerParams(vmem_limit_bytes=limit),
        cost_estimate=pl.CostEstimate(flops=flops, bytes_accessed=moved, transcendentals=0),
    )(*operands)


def normalize_body(down_ref, up_ref, first_ref, later_ref, up_out_ref):
    down = normalized(down_ref[...].astype(jnp.float32))[0].astype(jnp.bfloat16)
    up = normalized(up_ref[...].astype(jnp.float32))[0].astype(jnp.bfloat16)
    first_ref[0] = down[0]
    first_ref[1] = up[0]
    later_ref[0] = down[1]
    later_ref[1] = down[2]
    later_ref[2] = up[1]
    later_ref[3] = up[2]
    up_out_ref[...] = up


def forward_body(picks, h_ref, w_ref, *outs):
    count = len(picks)
    rows = h_ref.shape[0] * h_ref.shape[2]
    features = h_ref.shape[3]
    local = w_ref.shape[2]
    blocks = [h_ref[:, pick].reshape(rows, features) for pick in picks]
    hidden = blocks[0] if count == 1 else jnp.concatenate(blocks, axis=0)
    queries, keys, values = [dot_nn(hidden, w_ref[part]).astype(jnp.bfloat16) for part in range(3)]
    causal = lax.broadcasted_iota(jnp.int32, (rows, rows), 0) >= lax.broadcasted_iota(
        jnp.int32, (rows, rows), 1
    )
    for index in range(count):
        qkv_ref, soft_ref, a_ref = outs[3 * index : 3 * index + 3]
        span = slice(index * rows, (index + 1) * rows)
        for part, full in enumerate((queries, keys, values)):
            qkv_ref[part] = full[span]
        for head in range(local // HEAD):
            cols = slice(head * HEAD, (head + 1) * HEAD)
            scores = dot_nt(queries[span, cols], keys[span, cols]) * HEAD ** (-0.5)
            scores = jnp.where(causal, scores, -jnp.inf)
            powers = jnp.exp(scores - jnp.max(scores, axis=-1, keepdims=True))
            soft = powers / jnp.sum(powers, axis=-1, keepdims=True)
            soft_ref[head] = soft
            a_ref[:, cols] = dot_nn(soft.astype(jnp.bfloat16), values[span, cols]).astype(
                jnp.bfloat16
            )


def forward(hidden, picks, weights):
    rows = hidden.shape[0] * hidden.shape[2]
    features, local = weights.shape[1:]
    heads = local // HEAD
    one = [
        jax.ShapeDtypeStruct((3, rows, local), jnp.bfloat16),
        jax.ShapeDtypeStruct((heads, rows, rows), jnp.float32),
        jax.ShapeDtypeStruct((rows, local), jnp.bfloat16),
    ]
    count = len(picks)
    outs = local_call(
        functools.partial(forward_body, picks),
        one * count,
        (hidden, weights),
        flops=2 * count * rows * features * 3 * local,
        moved=4 * MIB,
    )
    return [outs[3 * index : 3 * index + 3] for index in range(count)]


def backward_body(g_ref, qkv_ref, soft_ref, a_ref, w_ref, o_ref, part_ref, factor_ref):
    shards, shard_rows, features = g_ref.shape
    rows = shards * shard_rows
    local = o_ref.shape[0]
    upstream = g_ref[...].reshape(rows, features)
    d_attended = dot_nt(upstream, o_ref[...]).astype(jnp.bfloat16)
    d_queries, d_keys, d_values = [], [], []
    for head in range(local // HEAD):
        cols = slice(head * HEAD, (head + 1) * HEAD)
        queries, keys, values = [qkv_ref[part, :, cols] for part in range(3)]
        soft = soft_ref[head]
        d_here = d_attended[:, cols]
        d_values.append(dot_tn(soft.astype(jnp.bfloat16), d_here).astype(jnp.bfloat16))
        d_probs = dot_nt(d_here, values)
        offset = jnp.sum(
            d_here.astype(jnp.float32) * a_ref[:, cols].astype(jnp.float32), axis=-1, keepdims=True
        )
        d_scores = (soft * (d_probs - offset) * HEAD ** (-0.5)).astype(jnp.bfloat16)
        d_queries.append(dot_nn(d_scores, keys).astype(jnp.bfloat16))
        d_keys.append(dot_tn(d_scores, queries).astype(jnp.bfloat16))
    pieces = [jnp.concatenate(parts, axis=1) for parts in (d_queries, d_keys, d_values)]
    for part in range(3):
        factor_ref[part] = pieces[part]
    factor_ref[3] = a_ref[...]
    tile = 512
    for start in range(0, features, tile):
        total = dot_nt(pieces[0], w_ref[0, start : start + tile, :])
        total += dot_nt(pieces[1], w_ref[1, start : start + tile, :])
        total += dot_nt(pieces[2], w_ref[2, start : start + tile, :])
        part_ref[:, :, start : start + tile] = total.astype(jnp.bfloat16).reshape(
            shards, shard_rows, tile
        )


def backward(gathered, saved, weights, weights_out):
    shards, shard_rows, features = gathered.shape
    rows = shards * shard_rows
    local = weights_out.shape[0]
    return local_call(
        backward_body,
        [
            jax.ShapeDtypeStruct((shards, shard_rows, features), jnp.bfloat16),
            jax.ShapeDtypeStruct((4, rows, local), jnp.bfloat16),
        ],
        (gathered, *saved, weights, weights_out),
        flops=2 * rows * features * 4 * local,
        moved=6 * MIB,
    )


def layer_back_body(other_end, parts_ref, x_ref, g_ref, loss_ref, y_ref):
    summed = jnp.sum(parts_ref[...].astype(jnp.float32), axis=0)
    normed, inverse = normalized(x_ref[...].astype(jnp.float32))
    backward = inverse * (
        summed
        - jnp.mean(summed, axis=-1, keepdims=True)
        - normed * jnp.mean(summed * normed, axis=-1, keepdims=True)
    )
    result = (g_ref[...].astype(jnp.float32) + backward).astype(jnp.bfloat16)
    if other_end is not None:
        result = jnp.where(lax.axis_index("section") == other_end, loss_ref[...], result)
    y_ref[...] = result


def layer_back(parts, stored, upstream, loss, other_end):
    return local_call(
        functools.partial(layer_back_body, other_end),
        jax.ShapeDtypeStruct(upstream.shape, jnp.bfloat16),
        (parts, stored, upstream, loss),
        flops=20 * parts.size,
        moved=2 * parts.size,
    )


def gradients_body(h0, later, mirrored, g0, g1, g2, n1, n2, *rest):
    factors, (w_ref, o_ref, d_all, a_all) = rest[:6], rest[6:]
    rows = factors[0].shape[1]

    @pl.when(pl.program_id(0) == 0)
    def _():
        for index, factor in enumerate(factors):
            for part in range(3):
                d_all[part, index * rows : (index + 1) * rows, :] = factor[part]
            a_all[:, index * rows : (index + 1) * rows] = factor[3].T

    tile = h0.shape[-1]

    def flat(block):
        return block.reshape(rows, tile)

    hidden = jnp.concatenate(
        [flat(h0[:, 0]), flat(later[:, 0]), flat(later[:, 1])]
        + [flat(mirrored[:, index]) for index in range(3)],
        axis=0,
    )
    upstream = jnp.concatenate(
        [flat(g0[...]), flat(g1[...]), flat(g2[...]), flat(mirrored[:, 3]), flat(n1[...]), flat(n2[...])],
        axis=0,
    )
    turned = hidden.T
    for part in range(3):
        w_ref[part] = dot_nn(turned, d_all[part]).astype(jnp.bfloat16)
    o_ref[...] = dot_nn(a_all[...], upstream).astype(jnp.bfloat16)


def gradients(first, later, mirrored, flows, mirrored_flows, factors, mirrored_factors):
    features = first.shape[-1]
    rows, local = factors[0].shape[1:]
    tile = 256
    shards = first.shape[0]
    shard_rows = first.shape[2]

    def four(count):
        return pl.BlockSpec((shards, count, shard_rows, tile), lambda i: (0, 0, 0, i))

    three = pl.BlockSpec((shards, shard_rows, tile), lambda i: (0, 0, i))
    whole = pl.BlockSpec((4, rows, local), lambda i: (0, 0, 0))
    depth = 6 * rows
    return pl.pallas_call(
        gradients_body,
        grid=(features // tile,),
        out_shape=[
            jax.ShapeDtypeStruct((3, features, local), jnp.bfloat16),
            jax.ShapeDtypeStruct((local, features), jnp.bfloat16),
        ],
        in_specs=[four(1), four(2), four(4)] + [three] * 5 + [whole] * 6,
        out_specs=[
            pl.BlockSpec((3, tile, local), lambda i: (0, i, 0)),
            pl.BlockSpec((local, tile), lambda i: (0, i)),
        ],
        scratch_shapes=[
            pltpu.VMEM((3, depth, local), jnp.bfloat16),
            pltpu.VMEM((local, depth), jnp.bfloat16),
        ],
        compiler_params=pltpu.CompilerParams(vmem_limit_bytes=24 * MIB),
        cost_estimate=pl.CostEstimate(
            flops=2 * depth * features * 4 * local, bytes_accessed=12 * MIB, transcendentals=0
        ),
    )(first, later, mirrored, *flows, *mirrored_flows, *factors, *mirrored_factors)


def spread(rows):
    count = lax.axis_size("tp")
    return lax.all_to_all(
        jnp.broadcast_to(rows[None], (count,) + rows.shape), "tp", split_axis=0, concat_axis=0, tiled=True
    )


def exchanged(parts):
    return lax.all_to_all(parts, "tp", split_axis=0, concat_axis=0, tiled=True)


def per_device(
    query_key_value_weight,
    output_weight,
    ascending_query_key_value_weight,
    ascending_output_weight,
    descending_saved_input,
    ascending_saved_input,
    descending_transit_gradient,
    ascending_transit_gradient,
    descending_loss_gradient,
    ascending_loss_gradient,
):
    sections = lax.axis_size("section")
    last = sections - 1
    w_down = jnp.transpose(query_key_value_weight[0], (1, 0, 2))
    w_up = jnp.transpose(ascending_query_key_value_weight[0], (1, 0, 2))
    o_down = output_weight[0]
    o_up = ascending_output_weight[0]
    x_down = descending_saved_input[0]
    x_up = ascending_saved_input[0]
    flow_down = descending_transit_gradient[0]
    flow_up = ascending_transit_gradient[0]
    shard_rows, features = flow_up.shape

    lower = [(index, (index - 1) % sections) for index in range(sections)]
    upper = [(index, (index + 1) % sections) for index in range(sections)]
    across = [(index, last - index) for index in range(sections)]
    upper_across = [(index, last - (index + 1) % sections) for index in range(sections)]

    h_first, h_later, h_up = local_call(
        normalize_body,
        [
            jax.ShapeDtypeStruct((2, shard_rows, features), jnp.bfloat16),
            jax.ShapeDtypeStruct((4, shard_rows, features), jnp.bfloat16),
            jax.ShapeDtypeStruct((TICKS, shard_rows, features), jnp.bfloat16),
        ],
        (x_down, x_up),
        flops=20 * x_up.size,
        moved=8 * x_up.size,
    )
    g_up = spread(flow_up)
    g_down = spread(flow_down)
    h0 = spread(h_first)
    later = lax.all_gather(h_later, "tp", axis=0, tiled=False)
    sent = lax.ppermute(jnp.concatenate([h_up, flow_up[None]], axis=0), "section", across)
    mirrored = lax.all_gather(sent, "tp", axis=0, tiled=False)

    saved_up = forward(h0, (1,), w_up)
    saved_down = forward(h0, (0,), w_down)
    flows, mirrored_flows, factors, mirrored_factors = [], [], [], []
    for tick in range(TICKS):
        if tick == 1:
            saved_up += forward(later, (2, 3), w_up)
            saved_down += forward(later, (0, 1), w_down)
        flows.append(g_down)
        final = tick + 1 == TICKS
        loss = min(tick, TICKS - 2)
        part_up, factor_up = backward(g_up, saved_up[tick], w_up, o_up)
        part_up = exchanged(part_up)
        mirrored_factors.append(lax.ppermute(factor_up, "section", across))
        part_down, factor_down = backward(g_down, saved_down[tick], w_down, o_down)
        part_down = exchanged(part_down)
        factors.append(factor_down)
        y_up = layer_back(
            part_up, x_up[tick], flow_up, ascending_loss_gradient[loss], None if final else last
        )
        y_down = layer_back(
            part_down, x_down[tick], flow_down, descending_loss_gradient[loss], None if final else 0
        )
        if not final:
            flow_up = lax.ppermute(y_up, "section", upper)
            flow_down = lax.ppermute(y_down, "section", lower)
            g_up = spread(flow_up)
            g_down = spread(flow_down)
            mirrored_flows.append(spread(lax.ppermute(y_up, "section", upper_across)))
    grad_qkv, grad_out = gradients(
        h0[:, :1], later, mirrored, flows, mirrored_flows, factors, mirrored_factors
    )
    return (
        jnp.transpose(grad_qkv, (1, 0, 2))[None],
        grad_out[None],
        y_down[None],
        y_up[None],
    )


def solution(mesh):
    in_specs = (
        P("section", None, None, "tp"),
        P("section", "tp", None),
        P("section", None, None, "tp"),
        P("section", "tp", None),
        P("section", None, "tp", None),
        P("section", None, "tp", None),
        P("section", "tp", None),
        P("section", "tp", None),
        P(None, "tp", None),
        P(None, "tp", None),
    )
    out_specs = (
        P("section", None, None, "tp"),
        P("section", "tp", None),
        P("section", "tp", None),
        P("section", "tp", None),
    )
    return jax.shard_map(
        per_device, mesh=mesh, in_specs=in_specs, out_specs=out_specs, check_vma=False
    )
```

profile of v0, /device:TPU:1, one launch (start us, length us, event | category | flops | bytes accessed | tf_op | source)
XLA Modules:
  0.0 313.6 jit_solution(3380429175128146816)
XLA Ops:
  8.9 6.0 %all-to-all-start.6 = ((bf16[8,16,2048]{2,1,0:T(8,128)(2,1)}), bf16[8,16,2048]{2,1,0:T(8,128)(2,1)}, u32[]{:S(2)}, u32[]{:S(2)}) async-start(bf16[8,16,2048]{2,1,0:T(8,128)(2,1)} %broadcast_in_dim.36), calls=%async_computation.6 | async-start | bytes 1048576 | tf_op jit(solution)/shard_map/all_to_all | solution.py:249
  18.7 6.4 %all-to-all-done.6.g_ref = bf16[8,16,2048]{2,1,0:T(8,128)(2,1)} async-done(((bf16[8,16,2048]{2,1,0:T(8,128)(2,1)}), bf16[8,16,2048]{2,1,0:T(8,128)(2,1)}, u32[]{:S(2)}, u32[]{:S(2)}) %all-to-all-start.6) | async-done | bytes 524320 | tf_op jit(solution)/shard_map/all_to_all | solution.py:249
  26.1 21.5 %all_to_all.75.h_ref = bf16[8,2,16,2048]{3,2,1,0:T(8,128)(2,1)} all-to-all(bf16[8,2,16,2048]{3,2,1,0:T(8,128)(2,1)S(1)} %broadcast_in_dim.30), channel_id=1, replica_groups=mesh['section'=32,'tp'=8] {'tp'}, dimensions={0} | all-to-all | bytes 2097152 | tf_op jit(solution)/shard_map/all_to_all | solution.py:249
  48.4 4.3 %all-to-all-start.1 = ((bf16[8,16,2048]{2,1,0:T(8,128)(2,1)}), bf16[8,16,2048]{2,1,0:T(8,128)(2,1)}, u32[]{:S(2)}, u32[]{:S(2)}) async-start(bf16[8,16,2048]{2,1,0:T(8,128)(2,1)} %broadcast_in_dim.32), calls=%async_computation.1 | async-start | bytes 1048576 | tf_op jit(solution)/shard_map/all_to_all | solution.py:249
  53.5 14.6 %collective-permute-start = (bf16[4,16,2048]{2,1,0:T(8,128)(2,1)}, bf16[4,16,2048]{2,1,0:T(8,128)(2,1)}, u32[]{:S(2)}, u32[]{:S(2)}) collective-permute-start(bf16[4,16,2048]{2,1,0:T(8,128)(2,1)} %pad_maximum_fusion), channel_id=1, source_target_pairs={{0,248},{8,240},{16,232},{24,224},{32,216},{40,208},{48,200},{56,1... | collective-permute-start | bytes 786440 | tf_op jit(solution)/shard_map/ppermute | solution.py:302
  70.7 3.7 %shard_map.137 = (bf16[8,16,2048]{2,1,0:T(8,128)(2,1)S(1)}, bf16[4,128,256]{2,1,0:T(8,128)(2,1)S(1)}) custom-call(bf16[8,16,2048]{2,1,0:T(8,128)(2,1)} %all-to-all-done.6.g_ref, bf16[3,128,256]{2,1,0:T(8,128)(2,1)S(1)} %get-tuple-element.50.qkv_ref, f32[2,128,128]{2,1,0:T(8,128)S(1)} %get-tuple-element.51.soft_ref, ...), custom_call_target="tpu_custom_call" | custom-call | flops 536870912 | bytes 6291456 | tf_op jit(solution)/shard_map/pallas_call | solution.py:36
  75.9 4.8 %all-to-all-start.7 = ((bf16[8,16,2048]{2,1,0:T(8,128)(2,1)}), bf16[8,16,2048]{2,1,0:T(8,128)(2,1)}, u32[]{:S(2)}, u32[]{:S(2)}) async-start(bf16[8,16,2048]{2,1,0:T(8,128)(2,1)} %copy-done.26), calls=%async_computation.7 | async-start | bytes 1048576 | tf_op jit(solution)/shard_map/all_to_all | solution.py:255
  83.9 3.6 %shard_map.131 = (bf16[8,16,2048]{2,1,0:T(8,128)(2,1)S(1)}, bf16[4,128,256]{2,1,0:T(8,128)(2,1)S(1)}) custom-call(bf16[8,16,2048]{2,1,0:T(8,128)(2,1)} %all-to-all-done.1.g_ref.g0, bf16[3,128,256]{2,1,0:T(8,128)(2,1)S(1)} %get-tuple-element.42.qkv_ref, f32[2,128,128]{2,1,0:T(8,128)S(1)} %get-tuple-element.43.soft_ref, ...), custom_call_target="tpu_custom_call" | custom-call | flops 536870912 | bytes 6291456 | tf_op jit(solution)/shard_map/pallas_call | solution.py:36
  89.6 4.6 %all-to-all-start.2 = ((bf16[8,16,2048]{2,1,0:T(8,128)(2,1)}), bf16[8,16,2048]{2,1,0:T(8,128)(2,1)}, u32[]{:S(2)}, u32[]{:S(2)}) async-start(bf16[8,16,2048]{2,1,0:T(8,128)(2,1)} %copy-done.27), calls=%async_computation.2 | async-start | bytes 1048576 | tf_op jit(solution)/shard_map/all_to_all | solution.py:255
  97.9 9.8 %collective-permute-start.3 = (bf16[16,2048]{1,0:T(8,128)(2,1)}, bf16[16,2048]{1,0:T(8,128)(2,1)S(1)}, u32[]{:S(2)}, u32[]{:S(2)}) collective-permute-start(bf16[16,2048]{1,0:T(8,128)(2,1)} %shard_map.138), channel_id=1, source_target_pairs={{0,240},{8,232},{16,224},{24,216},{32,208},{40,200},{48,192},{56,1... | collective-permute-start | bytes 196616 | tf_op jit(solution)/shard_map/ppermute | solution.py:332
  110.3 4.5 %all-to-all-start.8 = ((bf16[8,16,2048]{2,1,0:T(8,128)(2,1)}), bf16[8,16,2048]{2,1,0:T(8,128)(2,1)}, u32[]{:S(2)}, u32[]{:S(2)}) async-start(bf16[8,16,2048]{2,1,0:T(8,128)(2,1)} %broadcast_in_dim.37), calls=%async_computation.8 | async-start | bytes 1048576 | tf_op jit(solution)/shard_map/all_to_all | solution.py:249
  118.0 5.2 %collective-permute-start.1 = (bf16[16,2048]{1,0:T(8,128)(2,1)S(1)}, bf16[16,2048]{1,0:T(8,128)(2,1)S(1)}, u32[]{:S(2)}, u32[]{:S(2)}) collective-permute-start(bf16[16,2048]{1,0:T(8,128)(2,1)S(1)} %shard_map.132), channel_id=1, source_target_pairs={{0,248},{8,0},{16,8},{24,16},{32,24},{40,32},{48,40},{56,48},{64,5... | collective-permute-start | bytes 196616 | tf_op jit(solution)/shard_map/ppermute | solution.py:329
  127.1 5.0 %all-to-all-start.3 = ((bf16[8,16,2048]{2,1,0:T(8,128)(2,1)}), bf16[8,16,2048]{2,1,0:T(8,128)(2,1)}, u32[]{:S(2)}, u32[]{:S(2)}) async-start(bf16[8,16,2048]{2,1,0:T(8,128)(2,1)} %broadcast_in_dim.33), calls=%async_computation.3 | async-start | bytes 1048576 | tf_op jit(solution)/shard_map/all_to_all | solution.py:249
  137.0 4.9 %all-to-all-done.3.g_ref.g1 = bf16[8,16,2048]{2,1,0:T(8,128)(2,1)} async-done(((bf16[8,16,2048]{2,1,0:T(8,128)(2,1)}), bf16[8,16,2048]{2,1,0:T(8,128)(2,1)}, u32[]{:S(2)}, u32[]{:S(2)}) %all-to-all-start.3) | async-done | bytes 524320 | tf_op jit(solution)/shard_map/all_to_all | solution.py:249
  142.8 4.1 %all-to-all-start.9 = ((bf16[8,16,2048]{2,1,0:T(8,128)(2,1)}), bf16[8,16,2048]{2,1,0:T(8,128)(2,1)}, u32[]{:S(2)}, u32[]{:S(2)}) async-start(bf16[8,16,2048]{2,1,0:T(8,128)(2,1)} %broadcast_in_dim.76), calls=%async_computation.9 | async-start | bytes 1048576 | tf_op jit(solution)/shard_map/all_to_all | solution.py:249
  158.9 4.3 %all-to-all-start.4 = ((bf16[8,16,2048]{2,1,0:T(8,128)(2,1)}), bf16[8,16,2048]{2,1,0:T(8,128)(2,1)}, u32[]{:S(2)}, u32[]{:S(2)}) async-start(bf16[8,16,2048]{2,1,0:T(8,128)(2,1)} %copy-done.28), calls=%async_computation.4 | async-start | bytes 1048576 | tf_op jit(solution)/shard_map/all_to_all | solution.py:255
  170.9 3.6 %shard_map.140 = (bf16[8,16,2048]{2,1,0:T(8,128)(2,1)S(1)}, bf16[4,128,256]{2,1,0:T(8,128)(2,1)S(1)}) custom-call(bf16[8,16,2048]{2,1,0:T(8,128)(2,1)} %all-to-all-done.9.g_ref, bf16[3,128,256]{2,1,0:T(8,128)(2,1)S(1)} %get-tuple-element.54.qkv_ref, f32[2,128,128]{2,1,0:T(8,128)S(1)} %get-tuple-element.55.soft_ref, ...), custom_call_target="tpu_custom_call" | custom-call | flops 536870912 | bytes 6291456 | tf_op jit(solution)/shard_map/pallas_call | solution.py:36
  176.0 4.8 %all-to-all-start.10 = ((bf16[8,16,2048]{2,1,0:T(8,128)(2,1)}), bf16[8,16,2048]{2,1,0:T(8,128)(2,1)}, u32[]{:S(2)}, u32[]{:S(2)}) async-start(bf16[8,16,2048]{2,1,0:T(8,128)(2,1)} %copy-done.29), calls=%async_computation.10 | async-start | bytes 1048576 | tf_op jit(solution)/shard_map/all_to_all | solution.py:255
  182.8 3.7 %collective-permute-start.2 = (bf16[16,2048]{1,0:T(8,128)(2,1)}, bf16[16,2048]{1,0:T(8,128)(2,1)S(1)}, u32[]{:S(2)}, u32[]{:S(2)}) collective-permute-start(bf16[16,2048]{1,0:T(8,128)(2,1)} %shard_map.135), channel_id=1, source_target_pairs={{0,248},{8,0},{16,8},{24,16},{32,24},{40,32},{48,40},{56,48},{64,5... | collective-permute-start | bytes 196616 | tf_op jit(solution)/shard_map/ppermute | solution.py:329
  190.7 4.4 %all-to-all-start.5 = ((bf16[8,16,2048]{2,1,0:T(8,128)(2,1)}), bf16[8,16,2048]{2,1,0:T(8,128)(2,1)}, u32[]{:S(2)}, u32[]{:S(2)}) async-start(bf16[8,16,2048]{2,1,0:T(8,128)(2,1)} %broadcast_in_dim.34), calls=%async_computation.5 | async-start | bytes 1048576 | tf_op jit(solution)/shard_map/all_to_all | solution.py:249
  196.5 10.1 %collective-permute-start.5 = (bf16[16,2048]{1,0:T(8,128)(2,1)S(1)}, bf16[16,2048]{1,0:T(8,128)(2,1)S(1)}, u32[]{:S(2)}, u32[]{:S(2)}) collective-permute-start(bf16[16,2048]{1,0:T(8,128)(2,1)S(1)} %shard_map.141), channel_id=1, source_target_pairs={{0,240},{8,232},{16,224},{24,216},{32,208},{40,200},{48,192},{56,1... | collective-permute-start | bytes 196616 | tf_op jit(solution)/shard_map/ppermute | solution.py:332
  209.4 4.2 %all-to-all-start.11 = ((bf16[8,16,2048]{2,1,0:T(8,128)(2,1)}), bf16[8,16,2048]{2,1,0:T(8,128)(2,1)}, u32[]{:S(2)}, u32[]{:S(2)}) async-start(bf16[8,16,2048]{2,1,0:T(8,128)(2,1)} %broadcast_in_dim.77), calls=%async_computation.11 | async-start | bytes 1048576 | tf_op jit(solution)/shard_map/all_to_all | solution.py:249
  222.2 4.3 %all-to-all-start.12 = ((bf16[8,16,2048]{2,1,0:T(8,128)(2,1)}), bf16[8,16,2048]{2,1,0:T(8,128)(2,1)}, u32[]{:S(2)}, u32[]{:S(2)}) async-start(bf16[8,16,2048]{2,1,0:T(8,128)(2,1)} %broadcast_in_dim.78), calls=%async_computation.12 | async-start | bytes 1048576 | tf_op jit(solution)/shard_map/all_to_all | solution.py:249
  230.4 3.5 %shard_map.142 = (bf16[8,16,2048]{2,1,0:T(8,128)(2,1)S(1)}, bf16[4,128,256]{2,1,0:T(8,128)(2,1)S(1)}) custom-call(bf16[8,16,2048]{2,1,0:T(8,128)(2,1)} %all-to-all-done.5.g_ref.g2, bf16[3,128,256]{2,1,0:T(8,128)(2,1)S(1)} %copy-done.41, f32[2,128,128]{2,1,0:T(8,128)S(1)} %copy-done.45, bf16[128,256]{1,0:T(8,128)(2,1)S(1)} %copy-done.50, ...), custom_call_target="tpu_custom_call" | custom-call | flops 536870912 | bytes 6291456 | tf_op jit(solution)/shard_map/pallas_call | solution.py:36
  235.4 5.2 %all-to-all-start.13 = ((bf16[8,16,2048]{2,1,0:T(8,128)(2,1)}), bf16[8,16,2048]{2,1,0:T(8,128)(2,1)}, u32[]{:S(2)}, u32[]{:S(2)}) async-start(bf16[8,16,2048]{2,1,0:T(8,128)(2,1)} %copy-done.24), calls=%async_computation.13 | async-start | bytes 1048576 | tf_op jit(solution)/shard_map/all_to_all | solution.py:255
  240.6 11.8 %collective-permute-start.6 = (bf16[4,128,256]{2,1,0:T(8,128)(2,1)}, bf16[4,128,256]{2,1,0:T(8,128)(2,1)}, u32[]{:S(2)}, u32[]{:S(2)}) collective-permute-start(bf16[4,128,256]{2,1,0:T(8,128)(2,1)} %copy-done.52), channel_id=1, source_target_pairs={{0,248},{8,240},{16,232},{24,224},{32,216},{40,208},{48,200},{56,1... | collective-permute-start | bytes 786440 | tf_op jit(solution)/shard_map/ppermute | solution.py:317
  257.4 4.3 %shard_map.143 = (bf16[8,16,2048]{2,1,0:T(8,128)(2,1)S(1)}, bf16[4,128,256]{2,1,0:T(8,128)(2,1)}) custom-call(bf16[8,16,2048]{2,1,0:T(8,128)(2,1)} %all-to-all-done.12.g_ref, bf16[3,128,256]{2,1,0:T(8,128)(2,1)S(1)} %copy-done.39, f32[2,128,128]{2,1,0:T(8,128)S(1)} %copy-done.43, bf16[128,256]{1,0:T(8,128)(2,1)S(1)} %copy-done.48, ...), custom_call_target="tpu_custom_call" | custom-call | flops 536870912 | bytes 6291456 | tf_op jit(solution)/shard_map/pallas_call | solution.py:36
  262.5 5.3 %collective-permute-start.9 = (bf16[4,128,256]{2,1,0:T(8,128)(2,1)}, bf16[4,128,256]{2,1,0:T(8,128)(2,1)}, u32[]{:S(2)}, u32[]{:S(2)}) collective-permute-start(bf16[4,128,256]{2,1,0:T(8,128)(2,1)} %get-tuple-element.69), channel_id=1, source_target_pairs={{0,248},{8,240},{16,232},{24,224},{32,216},{40,208},{48,200},{56,1... | collective-permute-start | bytes 786440 | tf_op jit(solution)/shard_map/ppermute | solution.py:317
  267.8 4.8 %all-to-all-start.14 = ((bf16[8,16,2048]{2,1,0:T(8,128)(2,1)}), bf16[8,16,2048]{2,1,0:T(8,128)(2,1)}, u32[]{:S(2)}, u32[]{:S(2)}) async-start(bf16[8,16,2048]{2,1,0:T(8,128)(2,1)} %copy-done.23), calls=%async_computation.14 | async-start | bytes 1048576 | tf_op jit(solution)/shard_map/all_to_all | solution.py:255
  273.4 10.4 %collective-permute-done.7.rest_4_ = bf16[4,128,256]{2,1,0:T(8,128)(2,1)} collective-permute-done((bf16[4,128,256]{2,1,0:T(8,128)(2,1)}, bf16[4,128,256]{2,1,0:T(8,128)(2,1)}, u32[]{:S(2)}, u32[]{:S(2)}) %collective-permute-start.7) | collective-permute-done | bytes 262176 | tf_op jit(solution)/shard_map/ppermute | solution.py:317
  283.8 4.4 %collective-permute-done.9.rest_5_ = bf16[4,128,256]{2,1,0:T(8,128)(2,1)} collective-permute-done((bf16[4,128,256]{2,1,0:T(8,128)(2,1)}, bf16[4,128,256]{2,1,0:T(8,128)(2,1)}, u32[]{:S(2)}, u32[]{:S(2)}) %collective-permute-start.9) | collective-permute-done | bytes 262176 | tf_op jit(solution)/shard_map/ppermute | solution.py:317
  293.7 9.1 %shard_map.144 = (bf16[3,2048,256]{2,1,0:T(8,128)(2,1)}, bf16[256,2048]{1,0:T(8,128)(2,1)}) custom-call(bf16[8,1,16,2048]{3,2,1,0:T(8,128)(2,1)S(1)} %copy-done.25, bf16[8,4,16,2048]{3,2,1,0:T(8,128)(2,1)S(1)} %bitcast.58, bf16[8,4,16,2048]{3,2,1,0:T(8,128)(2,1)S(1)} %bitcast.65, bf16[8,16,2048]{2,1,0:T(8,128)(2,1)} %all-to-all-done.1.g_ref.g0, ...), custom_call_target="tpu_custom_call" | custom-call | flops 3221225472 | bytes 12582912 | tf_op jit(solution)/shard_map/pallas_call | solution.py:224
  (176 shorter events, 97.7 us)
Async XLA Ops:
  7.2 40.4 %copy-start.30 = (bf16[1,16,2048]{2,1,0:T(8,128)(2,1)S(1)}, bf16[1,16,2048]{2,1,0:T(8,128)(2,1)}, u32[]{:S(2)}) copy-start(bf16[1,16,2048]{2,1,0:T(8,128)(2,1)} %param.16) | copy-start | bytes 196612
  8.9 43.9 %copy-start.22 = (bf16[1,16,2048]{2,1,0:T(8,128)(2,1)S(1)}, bf16[1,16,2048]{2,1,0:T(8,128)(2,1)}, u32[]{:S(2)}) copy-start(bf16[1,16,2048]{2,1,0:T(8,128)(2,1)} %param.17) | copy-start | bytes 196612
  8.9 16.2 %all-to-all-start.6 = ((bf16[8,16,2048]{2,1,0:T(8,128)(2,1)}), bf16[8,16,2048]{2,1,0:T(8,128)(2,1)}, u32[]{:S(2)}, u32[]{:S(2)}) async-start(bf16[8,16,2048]{2,1,0:T(8,128)(2,1)} %broadcast_in_dim.36), calls=%async_computation.6 | async-start | bytes 1048576 | tf_op jit(solution)/shard_map/all_to_all | solution.py:249
  14.9 53.2 %copy-start.1 = (bf16[1,2048,3,256]{3,1,2,0:T(8,128)(2,1)S(1)}, bf16[1,2048,3,256]{3,1,2,0:T(8,128)(2,1)}, u32[]{:S(2)}) copy-start(bf16[1,2048,3,256]{3,1,2,0:T(8,128)(2,1)} %param.12) | copy-start | bytes 9437188
  14.9 132.1 %all-gather.5.cloned.1.call-start = ((), (), s32[]{:S(2)}) async-start(), calls=%async_computation.15 | async-start | bytes 2359296 | tf_op jit(solution)/shard_map/all_gather | solution.py:301
  48.4 27.5 %all-to-all-start.1 = ((bf16[8,16,2048]{2,1,0:T(8,128)(2,1)}), bf16[8,16,2048]{2,1,0:T(8,128)(2,1)}, u32[]{:S(2)}, u32[]{:S(2)}) async-start(bf16[8,16,2048]{2,1,0:T(8,128)(2,1)} %broadcast_in_dim.32), calls=%async_computation.1 | async-start | bytes 1048576 | tf_op jit(solution)/shard_map/all_to_all | solution.py:249
  53.5 78.7 %collective-permute-start = (bf16[4,16,2048]{2,1,0:T(8,128)(2,1)}, bf16[4,16,2048]{2,1,0:T(8,128)(2,1)}, u32[]{:S(2)}, u32[]{:S(2)}) collective-permute-start(bf16[4,16,2048]{2,1,0:T(8,128)(2,1)} %pad_maximum_fusion), channel_id=1, source_target_pairs={{0,248},{8,240},{16,232},{24,224},{32,216},{40,208},{48,200},{56,1... | collective-permute-start | bytes 786440 | tf_op jit(solution)/shard_map/ppermute | solution.py:302
  75.9 13.7 %all-to-all-start.7 = ((bf16[8,16,2048]{2,1,0:T(8,128)(2,1)}), bf16[8,16,2048]{2,1,0:T(8,128)(2,1)}, u32[]{:S(2)}, u32[]{:S(2)}) async-start(bf16[8,16,2048]{2,1,0:T(8,128)(2,1)} %copy-done.26), calls=%async_computation.7 | async-start | bytes 1048576 | tf_op jit(solution)/shard_map/all_to_all | solution.py:255
  89.6 18.8 %all-to-all-start.2 = ((bf16[8,16,2048]{2,1,0:T(8,128)(2,1)}), bf16[8,16,2048]{2,1,0:T(8,128)(2,1)}, u32[]{:S(2)}, u32[]{:S(2)}) async-start(bf16[8,16,2048]{2,1,0:T(8,128)(2,1)} %copy-done.27), calls=%async_computation.2 | async-start | bytes 1048576 | tf_op jit(solution)/shard_map/all_to_all | solution.py:255
  97.9 11.6 %collective-permute-start.3 = (bf16[16,2048]{1,0:T(8,128)(2,1)}, bf16[16,2048]{1,0:T(8,128)(2,1)S(1)}, u32[]{:S(2)}, u32[]{:S(2)}) collective-permute-start(bf16[16,2048]{1,0:T(8,128)(2,1)} %shard_map.138), channel_id=1, source_target_pairs={{0,240},{8,232},{16,224},{24,216},{32,208},{40,200},{48,192},{56,1... | collective-permute-start | bytes 196616 | tf_op jit(solution)/shard_map/ppermute | solution.py:332
  110.3 15.9 %all-to-all-start.8 = ((bf16[8,16,2048]{2,1,0:T(8,128)(2,1)}), bf16[8,16,2048]{2,1,0:T(8,128)(2,1)}, u32[]{:S(2)}, u32[]{:S(2)}) async-start(bf16[8,16,2048]{2,1,0:T(8,128)(2,1)} %broadcast_in_dim.37), calls=%async_computation.8 | async-start | bytes 1048576 | tf_op jit(solution)/shard_map/all_to_all | solution.py:249
  118.0 8.3 %collective-permute-start.1 = (bf16[16,2048]{1,0:T(8,128)(2,1)S(1)}, bf16[16,2048]{1,0:T(8,128)(2,1)S(1)}, u32[]{:S(2)}, u32[]{:S(2)}) collective-permute-start(bf16[16,2048]{1,0:T(8,128)(2,1)S(1)} %shard_map.132), channel_id=1, source_target_pairs={{0,248},{8,0},{16,8},{24,16},{32,24},{40,32},{48,40},{56,48},{64,5... | collective-permute-start | bytes 196616 | tf_op jit(solution)/shard_map/ppermute | solution.py:329
  127.1 14.8 %all-to-all-start.3 = ((bf16[8,16,2048]{2,1,0:T(8,128)(2,1)}), bf16[8,16,2048]{2,1,0:T(8,128)(2,1)}, u32[]{:S(2)}, u32[]{:S(2)}) async-start(bf16[8,16,2048]{2,1,0:T(8,128)(2,1)} %broadcast_in_dim.33), calls=%async_computation.3 | async-start | bytes 1048576 | tf_op jit(solution)/shard_map/all_to_all | solution.py:249
  132.1 141.3 %all-gather.7.cloned.1.call-start = ((), (), s32[]{:S(2)}) async-start(), calls=%async_computation.16 | async-start | bytes 2359296 | tf_op jit(solution)/shard_map/all_gather | solution.py:303
  132.9 4.1 %collective-permute-start.4 = (bf16[16,2048]{1,0:T(8,128)(2,1)}, bf16[16,2048]{1,0:T(8,128)(2,1)S(1)}, u32[]{:S(2)}, u32[]{:S(2)}) collective-permute-start(bf16[16,2048]{1,0:T(8,128)(2,1)} %shard_map.138), channel_id=1, source_target_pairs={{0,8},{8,16},{16,24},{24,32},{32,40},{40,48},{48,56},{56,64},{64,7... | collective-permute-start | bytes 196616 | tf_op jit(solution)/shard_map/ppermute | solution.py:328
  142.8 16.1 %all-to-all-start.9 = ((bf16[8,16,2048]{2,1,0:T(8,128)(2,1)}), bf16[8,16,2048]{2,1,0:T(8,128)(2,1)}, u32[]{:S(2)}, u32[]{:S(2)}) async-start(bf16[8,16,2048]{2,1,0:T(8,128)(2,1)} %broadcast_in_dim.76), calls=%async_computation.9 | async-start | bytes 1048576 | tf_op jit(solution)/shard_map/all_to_all | solution.py:249
  158.9 17.1 %all-to-all-start.4 = ((bf16[8,16,2048]{2,1,0:T(8,128)(2,1)}), bf16[8,16,2048]{2,1,0:T(8,128)(2,1)}, u32[]{:S(2)}, u32[]{:S(2)}) async-start(bf16[8,16,2048]{2,1,0:T(8,128)(2,1)} %copy-done.28), calls=%async_computation.4 | async-start | bytes 1048576 | tf_op jit(solution)/shard_map/all_to_all | solution.py:255
  176.0 13.8 %all-to-all-start.10 = ((bf16[8,16,2048]{2,1,0:T(8,128)(2,1)}), bf16[8,16,2048]{2,1,0:T(8,128)(2,1)}, u32[]{:S(2)}, u32[]{:S(2)}) async-start(bf16[8,16,2048]{2,1,0:T(8,128)(2,1)} %copy-done.29), calls=%async_computation.10 | async-start | bytes 1048576 | tf_op jit(solution)/shard_map/all_to_all | solution.py:255
  182.8 7.0 %collective-permute-start.2 = (bf16[16,2048]{1,0:T(8,128)(2,1)}, bf16[16,2048]{1,0:T(8,128)(2,1)S(1)}, u32[]{:S(2)}, u32[]{:S(2)}) collective-permute-start(bf16[16,2048]{1,0:T(8,128)(2,1)} %shard_map.135), channel_id=1, source_target_pairs={{0,248},{8,0},{16,8},{24,16},{32,24},{40,32},{48,40},{56,48},{64,5... | collective-permute-start | bytes 196616 | tf_op jit(solution)/shard_map/ppermute | solution.py:329
  190.7 17.9 %all-to-all-start.5 = ((bf16[8,16,2048]{2,1,0:T(8,128)(2,1)}), bf16[8,16,2048]{2,1,0:T(8,128)(2,1)}, u32[]{:S(2)}, u32[]{:S(2)}) async-start(bf16[8,16,2048]{2,1,0:T(8,128)(2,1)} %broadcast_in_dim.34), calls=%async_computation.5 | async-start | bytes 1048576 | tf_op jit(solution)/shard_map/all_to_all | solution.py:249
  196.5 12.1 %collective-permute-start.5 = (bf16[16,2048]{1,0:T(8,128)(2,1)S(1)}, bf16[16,2048]{1,0:T(8,128)(2,1)S(1)}, u32[]{:S(2)}, u32[]{:S(2)}) collective-permute-start(bf16[16,2048]{1,0:T(8,128)(2,1)S(1)} %shard_map.141), channel_id=1, source_target_pairs={{0,240},{8,232},{16,224},{24,216},{32,208},{40,200},{48,192},{56,1... | collective-permute-start | bytes 196616 | tf_op jit(solution)/shard_map/ppermute | solution.py:332
  209.4 11.9 %all-to-all-start.11 = ((bf16[8,16,2048]{2,1,0:T(8,128)(2,1)}), bf16[8,16,2048]{2,1,0:T(8,128)(2,1)}, u32[]{:S(2)}, u32[]{:S(2)}) async-start(bf16[8,16,2048]{2,1,0:T(8,128)(2,1)} %broadcast_in_dim.77), calls=%async_computation.11 | async-start | bytes 1048576 | tf_op jit(solution)/shard_map/all_to_all | solution.py:249
  213.6 4.6 %collective-permute-start.8 = (bf16[16,2048]{1,0:T(8,128)(2,1)S(1)}, bf16[16,2048]{1,0:T(8,128)(2,1)S(1)}, u32[]{:S(2)}, u32[]{:S(2)}) collective-permute-start(bf16[16,2048]{1,0:T(8,128)(2,1)S(1)} %shard_map.141), channel_id=1, source_target_pairs={{0,8},{8,16},{16,24},{24,32},{32,40},{40,48},{48,56},{56,64},{64,7... | collective-permute-start | bytes 196616 | tf_op jit(solution)/shard_map/ppermute | solution.py:328
  222.2 30.3 %copy-start.43 = (f32[2,128,128]{2,1,0:T(8,128)S(1)}, f32[2,128,128]{2,1,0:T(8,128)}, u32[]{:S(2)}) copy-start(f32[2,128,128]{2,1,0:T(8,128)} %copy-done.42) | copy-start | bytes 393220
  222.2 13.3 %all-to-all-start.12 = ((bf16[8,16,2048]{2,1,0:T(8,128)(2,1)}), bf16[8,16,2048]{2,1,0:T(8,128)(2,1)}, u32[]{:S(2)}, u32[]{:S(2)}) async-start(bf16[8,16,2048]{2,1,0:T(8,128)(2,1)} %broadcast_in_dim.78), calls=%async_computation.12 | async-start | bytes 1048576 | tf_op jit(solution)/shard_map/all_to_all | solution.py:249
  235.4 37.1 %copy-start.8 = (bf16[8,2,16,2048]{3,2,1,0:T(8,128)(2,1)S(1)}, bf16[8,2,16,2048]{3,2,1,0:T(8,128)(2,1)}, u32[]{:S(2)}) copy-start(bf16[8,2,16,2048]{3,2,1,0:T(8,128)(2,1)} %all_to_all.75.h_ref) | copy-start | bytes 3145732
  235.4 32.3 %all-to-all-start.13 = ((bf16[8,16,2048]{2,1,0:T(8,128)(2,1)}), bf16[8,16,2048]{2,1,0:T(8,128)(2,1)}, u32[]{:S(2)}, u32[]{:S(2)}) async-start(bf16[8,16,2048]{2,1,0:T(8,128)(2,1)} %copy-done.24), calls=%async_computation.13 | async-start | bytes 1048576 | tf_op jit(solution)/shard_map/all_to_all | solution.py:255
  240.6 32.8 %collective-permute-start.6 = (bf16[4,128,256]{2,1,0:T(8,128)(2,1)}, bf16[4,128,256]{2,1,0:T(8,128)(2,1)}, u32[]{:S(2)}, u32[]{:S(2)}) collective-permute-start(bf16[4,128,256]{2,1,0:T(8,128)(2,1)} %copy-done.52), channel_id=1, source_target_pairs={{0,248},{8,240},{16,232},{24,224},{32,216},{40,208},{48,200},{56,1... | collective-permute-start | bytes 786440 | tf_op jit(solution)/shard_map/ppermute | solution.py:317
  252.4 31.4 %collective-permute-start.7 = (bf16[4,128,256]{2,1,0:T(8,128)(2,1)}, bf16[4,128,256]{2,1,0:T(8,128)(2,1)}, u32[]{:S(2)}, u32[]{:S(2)}) collective-permute-start(bf16[4,128,256]{2,1,0:T(8,128)(2,1)} %copy-done.57), channel_id=1, source_target_pairs={{0,248},{8,240},{16,232},{24,224},{32,216},{40,208},{48,200},{56,1... | collective-permute-start | bytes 786440 | tf_op jit(solution)/shard_map/ppermute | solution.py:317
  257.4 30.8 %copy-start.17 = (bf16[32,16,2048]{2,1,0:T(8,128)(2,1)S(1)}, bf16[32,16,2048]{2,1,0:T(8,128)(2,1)}, u32[]{:S(2)}) copy-start(bf16[32,16,2048]{2,1,0:T(8,128)(2,1)} %all-gather.5.cloned.1.call-done) | copy-start | bytes 6291460
  262.5 25.7 %collective-permute-start.9 = (bf16[4,128,256]{2,1,0:T(8,128)(2,1)}, bf16[4,128,256]{2,1,0:T(8,128)(2,1)}, u32[]{:S(2)}, u32[]{:S(2)}) collective-permute-start(bf16[4,128,256]{2,1,0:T(8,128)(2,1)} %get-tuple-element.69), channel_id=1, source_target_pairs={{0,248},{8,240},{16,232},{24,224},{32,216},{40,208},{48,200},{56,1... | collective-permute-start | bytes 786440 | tf_op jit(solution)/shard_map/ppermute | solution.py:317
  267.8 37.0 %all-to-all-start.14 = ((bf16[8,16,2048]{2,1,0:T(8,128)(2,1)}), bf16[8,16,2048]{2,1,0:T(8,128)(2,1)}, u32[]{:S(2)}, u32[]{:S(2)}) async-start(bf16[8,16,2048]{2,1,0:T(8,128)(2,1)} %copy-done.23), calls=%async_computation.14 | async-start | bytes 1048576 | tf_op jit(solution)/shard_map/all_to_all | solution.py:255
  (54 other events, 172.7 us)
Sparse Core Ops, SparseCore 0:
  18.8 57.5 all-gather.4
  134.7 51.3 all-gather.6
where the time goes:
time: 317 us; the launch traced here: 314 us
  starting transfers between devices  132 us (42%)
  local copies, waits for them, and re-layouts  51.7 us (16%)
  Pallas kernels  49.3 us (16%)
  waiting for transfers between devices  44 us (14%)
  blocking collectives  21.5 us (7%)
  between operations  14.5 us (5%)
    pallas_call x17, Pallas kernels, local_call(): pl.pallas_call(body, out_shape=out_shape, in_specs=[VMEM] * len(operands)...  40.2 us
    unnamed x120, local copies, waits for them, and re-layouts  39.1 us
    all_to_all x8, starting transfers between devices, spread(): lax.all_to_all(jnp.broadcast_to(rows[None], (count,) + rows.shape), 'tp',...  37 us
    all_to_all x6, starting transfers between devices, exchanged(): return lax.all_to_all(parts, 'tp', split_axis=0, concat_axis=0, tiled=True)  28.5 us
    all_to_all x1, blocking collectives, spread(): lax.all_to_all(jnp.broadcast_to(rows[None], (count,) + rows.shape), 'tp',...  21.5 us
    ppermute x2, starting transfers between devices, per_device(): mirrored_flows.append(spread(lax.ppermute(y_up, 'section', upper_across)))  19.9 us
    ppermute x3, starting transfers between devices, per_device(): mirrored_factors.append(lax.ppermute(factor_up, 'section', across))  17.2 us
    all_to_all x8, waiting for transfers between devices, spread(): lax.all_to_all(jnp.broadcast_to(rows[None], (count,) + rows.shape), 'tp',...  15.5 us
  transfers between devices with their start and end apart: 26, of which 13 were waited for; matrix products, arithmetic and copies ran while one was open for 4% of the time, Pallas kernels for 15%

commit v1 on v0

v1 whole, which is shorter than its diff:
```python
import functools

import jax
import jax.numpy as jnp
from jax import lax
from jax.experimental import pallas as pl
from jax.experimental.pallas import tpu as pltpu
from jax.sharding import PartitionSpec as P

HEAD = 128
TICKS = 3
EPSILON = 1e-05
MIB = 1 << 20
VMEM = pl.BlockSpec(memory_space=pltpu.VMEM)
ANY = pl.BlockSpec(memory_space=pl.ANY)
ROOM = 56 * MIB
CHUNK = 256


def dot_nn(left, right):
    return jnp.dot(left, right, preferred_element_type=jnp.float32)


def dot_nt(left, right):
    return lax.dot_general(left, right, (((1,), (1,)), ((), ())), preferred_element_type=jnp.float32)


def dot_tn(left, right):
    return lax.dot_general(left, right, (((0,), (0,)), ((), ())), preferred_element_type=jnp.float32)


def normalized(raw):
    centre = raw - jnp.mean(raw, axis=-1, keepdims=True)
    inverse = lax.rsqrt(jnp.mean(centre * centre, axis=-1, keepdims=True) + EPSILON)
    return centre * inverse, inverse


def local_call(body, out_shape, operands, flops, moved, in_specs=None, out_specs=None, scratch=()):
    return pl.pallas_call(
        body,
        out_shape=out_shape,
        in_specs=in_specs or [VMEM] * len(operands),
        out_specs=out_specs or jax.tree.map(lambda _: VMEM, out_shape),
        scratch_shapes=list(scratch),
        compiler_params=pltpu.CompilerParams(vmem_limit_bytes=ROOM),
        cost_estimate=pl.CostEstimate(flops=flops // 1000, bytes_accessed=moved // 1000, transcendentals=0),
    )(*operands)


def prepare_body(down_ref, up_ref, g_down_ref, g_up_ref, start_ref, later_ref, across_ref, block, sem):
    down = normalized(down_ref[...].astype(jnp.float32))[0].astype(jnp.bfloat16)
    up = normalized(up_ref[...].astype(jnp.float32))[0].astype(jnp.bfloat16)
    block[0] = up[0]
    block[1] = g_up_ref[...]
    block[2] = down[0]
    block[3] = g_down_ref[...]
    copies = [
        pltpu.make_async_copy(block, start_ref.at[shard], sem.at[shard])
        for shard in range(start_ref.shape[0])
    ]
    for copy in copies:
        copy.start()
    later_ref[0] = down[1]
    later_ref[1] = down[2]
    later_ref[2] = up[1]
    later_ref[3] = up[2]
    for tick in range(TICKS):
        across_ref[tick] = up[tick]
    across_ref[TICKS] = g_up_ref[...]
    for copy in copies:
        copy.wait()


def prepare(x_down, x_up, flow_down, flow_up):
    shards = lax.axis_size("tp")
    four = (4,) + flow_up.shape
    return local_call(
        prepare_body,
        [
            jax.ShapeDtypeStruct((shards,) + four, jnp.bfloat16),
            jax.ShapeDtypeStruct(four, jnp.bfloat16),
            jax.ShapeDtypeStruct(four, jnp.bfloat16),
        ],
        (x_down, x_up, flow_down, flow_up),
        flops=40 * x_up.size,
        moved=10 * x_up.size,
        out_specs=[ANY, VMEM, VMEM],
        scratch=[pltpu.VMEM(four, jnp.bfloat16), pltpu.SemaphoreType.DMA((shards,))],
    )


def repeat_body(*refs):
    sources, out_ref, sem = refs[:-2], refs[-2], refs[-1]
    copies = []
    for index, source in enumerate(sources):
        for shard in range(out_ref.shape[0]):
            copies.append(
                pltpu.make_async_copy(source, out_ref.at[shard, index], sem.at[index, shard])
            )
    for copy in copies:
        copy.start()
    for copy in copies:
        copy.wait()


def repeat(*rows):
    shards = lax.axis_size("tp")
    count = len(rows)
    return local_call(
        repeat_body,
        jax.ShapeDtypeStruct((shards, count) + rows[0].shape, jnp.bfloat16),
        rows,
        flops=rows[0].size,
        moved=16 * shards * rows[0].size,
        out_specs=ANY,
        scratch=[pltpu.SemaphoreType.DMA((count, shards))],
    )


def forward_body(picks, h_hbm, *refs):
    count = len(picks[0])
    weights, outs, (h_all, w_all, sem) = refs[:2], refs[2:-3], refs[-3:]
    features, local = w_all.shape[2:]
    rows = h_all.shape[2] * h_all.shape[3]
    h_copies = [
        [
            pltpu.make_async_copy(h_hbm.at[:, pick], h_all.at[pipe, index], sem.at[pipe, index])
            for index, pick in enumerate(picks[pipe])
        ]
        for pipe in range(2)
    ]
    w_copies = [
        [
            pltpu.make_async_copy(weights[pipe].at[part], w_all.at[pipe, part], sem.at[pipe, count + part])
            for part in range(3)
        ]
        for pipe in range(2)
    ]
    for pipe in range(2):
        for copy in h_copies[pipe] + w_copies[pipe]:
            copy.start()
    causal = lax.broadcasted_iota(jnp.int32, (rows, rows), 0) >= lax.broadcasted_iota(
        jnp.int32, (rows, rows), 1
    )
    for pipe in range(2):
        for copy in h_copies[pipe]:
            copy.wait()
        hidden = h_all[pipe].reshape(count * rows, features)
        projected = []
        for part in range(3):
            w_copies[pipe][part].wait()
            projected.append(dot_nn(hidden, w_all[pipe, part]).astype(jnp.bfloat16))
        queries, keys, values = projected
        for index in range(count):
            qkv_ref, soft_ref = outs[2 * index : 2 * index + 2]
            span = slice(index * rows, (index + 1) * rows)
            for part in range(3):
                qkv_ref[pipe, part] = projected[part][span]
            for head in range(local // HEAD):
                cols = slice(head * HEAD, (head + 1) * HEAD)
                scores = dot_nt(queries[span, cols], keys[span, cols]) * HEAD ** (-0.5)
                scores = jnp.where(causal, scores, -jnp.inf)
                powers = jnp.exp(scores - jnp.max(scores, axis=-1, keepdims=True))
                soft = powers / jnp.sum(powers, axis=-1, keepdims=True)
                soft_ref[pipe, head] = soft
                qkv_ref[pipe, 3, :, cols] = dot_nn(
                    soft.astype(jnp.bfloat16), values[span, cols]
                ).astype(jnp.bfloat16)


def forward(hidden, picks, w_up, w_down):
    shards, _, shard_rows, features = hidden.shape
    rows = shards * shard_rows
    local = w_up.shape[2]
    count = len(picks[0])
    outs = local_call(
        functools.partial(forward_body, picks),
        [
            jax.ShapeDtypeStruct((2, 4, rows, local), jnp.bfloat16),
            jax.ShapeDtypeStruct((2, local // HEAD, rows, rows), jnp.float32),
        ]
        * count,
        (hidden, w_up, w_down),
        flops=12 * count * rows * features * local,
        moved=8 * MIB,
        in_specs=[ANY] * 3,
        scratch=[
            pltpu.VMEM((2, count, shards, shard_rows, features), jnp.bfloat16),
            pltpu.VMEM((2, 3, features, local), jnp.bfloat16),
            pltpu.SemaphoreType.DMA((2, count + 3)),
        ],
    )
    return [outs[2 * index : 2 * index + 2] for index in range(count)]


def backward_body(picks, extra, g_hbm, qkv_hbm, soft_hbm, w_up, w_down, o_up, o_down, *rest):
    added, rest = rest[:extra], rest[extra:]
    part_hbm, factor_up, factor_down = rest[:3]
    g_all, qkv, soft_all, w_all, o_all, out, factor, sem, out_sem = rest[3:]
    shards, shard_rows, features = g_all.shape[1:]
    rows = shards * shard_rows
    local = o_all.shape[1]
    tile = 512
    copy = pltpu.make_async_copy
    first, second = [], []
    for pipe in range(2):
        first.append(
            [
                copy(g_hbm.at[:, picks[pipe]], g_all.at[pipe], sem.at[pipe, 0]),
                copy((o_up, o_down)[pipe], o_all.at[pipe], sem.at[pipe, 1]),
                copy(qkv_hbm.at[pipe], qkv.at[pipe], sem.at[pipe, 2]),
                copy(soft_hbm.at[pipe], soft_all.at[pipe], sem.at[pipe, 3]),
            ]
        )
        second.append([copy((w_up, w_down)[pipe], w_all.at[pipe], sem.at[pipe, 4])])
    for group in first + second:
        for one in group:
            one.start()
    pieces = []
    sent = [
        copy(row, part_hbm.at[shard, 2], out_sem.at[0, 1 + features // tile + shard])
        for row in added
        for shard in range(shards)
    ]
    for one in sent:
        one.start()
    for pipe in range(2):
        for one in first[pipe]:
            one.wait()
        upstream = g_all[pipe].reshape(rows, features)
        d_attended = dot_nt(upstream, o_all[pipe]).astype(jnp.bfloat16)
        d_queries, d_keys, d_values = [], [], []
        for head in range(local // HEAD):
            cols = slice(head * HEAD, (head + 1) * HEAD)
            queries, keys, values, attended = [qkv[pipe, part, :, cols] for part in range(4)]
            soft = soft_all[pipe, head]
            d_here = d_attended[:, cols]
            d_values.append(dot_tn(soft.astype(jnp.bfloat16), d_here).astype(jnp.bfloat16))
            d_probs = dot_nt(d_here, values)
            offset = jnp.sum(
                d_here.astype(jnp.float32) * attended.astype(jnp.float32), axis=-1, keepdims=True
            )
            d_scores = (soft * (d_probs - offset) * HEAD ** (-0.5)).astype(jnp.bfloat16)
            d_queries.append(dot_nn(d_scores, keys).astype(jnp.bfloat16))
            d_keys.append(dot_tn(d_scores, queries).astype(jnp.bfloat16))
        pieces.append([jnp.concatenate(parts, axis=1) for parts in (d_queries, d_keys, d_values)])
        for part in range(3):
            factor[pipe, part] = pieces[pipe][part]
        factor[pipe, 3] = qkv[pipe, 3]
        sent.append(copy(factor.at[pipe], (factor_up, factor_down)[pipe], out_sem.at[pipe, 0]))
        sent[-1].start()
    for pipe in range(2):
        for one in second[pipe]:
            one.wait()
        for index in range(features // tile):
            cols = slice(index * tile, (index + 1) * tile)
            total = dot_nt(pieces[pipe][0], w_all[pipe, 0, cols, :])
            total += dot_nt(pieces[pipe][1], w_all[pipe, 1, cols, :])
            total += dot_nt(pieces[pipe][2], w_all[pipe, 2, cols, :])
            out[pipe, :, :, cols] = total.astype(jnp.bfloat16).reshape(shards, shard_rows, tile)
            sent.append(
                copy(out.at[pipe, :, :, cols], part_hbm.at[:, pipe, :, cols], out_sem.at[pipe, 1 + index])
            )
            sent[-1].start()
    for one in sent:
        one.wait()


def backward(gathered, picks, saved, w_up, w_down, o_up, o_down, added):
    local, features = o_up.shape
    rows = saved[0].shape[2]
    shards = lax.axis_size("tp")
    wide = (shards, rows // shards, features)
    return local_call(
        functools.partial(backward_body, picks, len(added)),
        [
            jax.ShapeDtypeStruct((shards, 2 + len(added)) + wide[1:], jnp.bfloat16),
            jax.ShapeDtypeStruct((4, rows, local), jnp.bfloat16),
            jax.ShapeDtypeStruct((4, rows, local), jnp.bfloat16),
        ],
        (gathered, *saved, w_up, w_down, o_up, o_down, *added),
        flops=16 * rows * features * local,
        moved=12 * MIB,
        in_specs=[ANY] * 7 + [VMEM] * len(added),
        out_specs=[ANY] * 3,
        scratch=[
            pltpu.VMEM((2,) + wide, jnp.bfloat16),
            pltpu.VMEM((2, 4, rows, local), jnp.bfloat16),
            pltpu.VMEM((2, local // HEAD, rows, rows), jnp.float32),
            pltpu.VMEM((2, 3, features, local), jnp.bfloat16),
            pltpu.VMEM((2, local, features), jnp.bfloat16),
            pltpu.VMEM((2,) + wide, jnp.bfloat16),
            pltpu.VMEM((2, 4, rows, local), jnp.bfloat16),
            pltpu.SemaphoreType.DMA((2, 5)),
            pltpu.SemaphoreType.DMA((2, 1 + features // 512 + shards)),
        ],
    )


def layer_back_body(tick, ends, parts_ref, *refs):
    for pipe in range(2):
        x_ref, g_ref, loss_ref = refs[3 * pipe : 3 * pipe + 3]
        y_ref = refs[6 + pipe]
        summed = jnp.sum(parts_ref[:, pipe].astype(jnp.float32), axis=0)
        normed, inverse = normalized(x_ref[tick].astype(jnp.float32))
        backward = inverse * (
            summed
            - jnp.mean(summed, axis=-1, keepdims=True)
            - normed * jnp.mean(summed * normed, axis=-1, keepdims=True)
        )
        result = (g_ref[...].astype(jnp.float32) + backward).astype(jnp.bfloat16)
        if ends is not None:
            at_end = lax.axis_index("section") == ends[pipe]
            result = jnp.where(at_end, loss_ref[tick], result)
        y_ref[...] = result


def layer_back(parts, up, down, tick, ends):
    like = jax.ShapeDtypeStruct(up[1].shape, jnp.bfloat16)
    return local_call(
        functools.partial(layer_back_body, tick, ends),
        [like, like],
        (parts, *up, *down),
        flops=20 * parts.size,
        moved=3 * parts.size,
    )


def gradients_body(start, later, mirrored, g1, g2, moved, *rest):
    factors = rest[:6]
    w_ref, o_ref, d_all, a_all = rest[6:]
    rows = factors[0].shape[1]
    tile = start.shape[-1]

    @pl.when(pl.program_id(0) == 0)
    def _():
        for index, factor in enumerate(factors):
            for part in range(3):
                d_all[part, index * rows : (index + 1) * rows, :] = factor[part]
            a_all[:, index * rows : (index + 1) * rows] = factor[3].T

    def flat(block):
        return block.reshape(rows, tile)

    hidden = jnp.concatenate(
        [flat(start[:, 0]), flat(later[:, 0]), flat(later[:, 1])]
        + [flat(mirrored[:, index]) for index in range(TICKS)],
        axis=0,
    )
    upstream = jnp.concatenate(
        [flat(start[:, 1]), flat(g1[:, 0]), flat(g2[:, 0])]
        + [flat(mirrored[:, TICKS]), flat(mirrored[:, TICKS + 1]), flat(moved[:, 0])],
        axis=0,
    )
    turned = hidden.T
    for part in range(3):
        w_ref[part] = dot_nn(turned, d_all[part]).astype(jnp.bfloat16)
    o_ref[...] = dot_nn(a_all[...], upstream).astype(jnp.bfloat16)


def gradients(start, later, mirrored, gathered, moved, factors):
    features = start.shape[-1]
    rows, local = factors[0].shape[1:]
    tile = 256
    shards = start.shape[0]
    shard_rows = start.shape[2]

    def columns(count, at=0):
        return pl.BlockSpec((shards, count, shard_rows, tile), lambda i: (0, at, 0, i))

    whole = pl.BlockSpec((4, rows, local), lambda i: (0, 0, 0))
    depth = 2 * TICKS * rows
    return pl.pallas_call(
        gradients_body,
        grid=(features // tile,),
        out_shape=[
            jax.ShapeDtypeStruct((3, features, local), jnp.bfloat16),
            jax.ShapeDtypeStruct((local, features), jnp.bfloat16),
        ],
        in_specs=[columns(2, 1), columns(2), columns(TICKS + 2), columns(1, 1), columns(1, 1), columns(1, 2)] + [whole] * 6,
        out_specs=[
            pl.BlockSpec((3, tile, local), lambda i: (0, i, 0)),
            pl.BlockSpec((local, tile), lambda i: (0, i)),
        ],
        scratch_shapes=[
            pltpu.VMEM((3, depth, local), jnp.bfloat16),
            pltpu.VMEM((local, depth), jnp.bfloat16),
        ],
        compiler_params=pltpu.CompilerParams(vmem_limit_bytes=ROOM),
        cost_estimate=pl.CostEstimate(
            flops=2 * depth * features * 4 * local, bytes_accessed=12 * MIB, transcendentals=0
        ),
    )(start, later, mirrored, *gathered, moved, *factors)


def after(value, *others):
    return lax.optimization_barrier((value,) + others)[0]


def exchanged(parts):
    return lax.all_to_all(parts, "tp", split_axis=0, concat_axis=0, tiled=True)


def gathered_rows(rows):
    return lax.all_gather(rows, "tp", axis=0, tiled=False)


def per_device(
    query_key_value_weight,
    output_weight,
    ascending_query_key_value_weight,
    ascending_output_weight,
    descending_saved_input,
    ascending_saved_input,
    descending_transit_gradient,
    ascending_transit_gradient,
    descending_loss_gradient,
    ascending_loss_gradient,
):
    sections = lax.axis_size("section")
    last = sections - 1
    w_down = jnp.transpose(query_key_value_weight[0], (1, 0, 2))
    w_up = jnp.transpose(ascending_query_key_value_weight[0], (1, 0, 2))
    o_down = output_weight[0]
    o_up = ascending_output_weight[0]
    x_down = descending_saved_input[0]
    x_up = ascending_saved_input[0]
    flow_down = descending_transit_gradient[0]
    flow_up = ascending_transit_gradient[0]

    lower = [(index, (index - 1) % sections) for index in range(sections)]
    upper = [(index, (index + 1) % sections) for index in range(sections)]
    across = [(index, last - index) for index in range(sections)]

    start, h_later, sent = prepare(x_down, x_up, flow_down, flow_up)
    start = exchanged(start)
    start, h_later, sent = lax.optimization_barrier((start, h_later, sent))
    later = gathered_rows(h_later)
    sent = lax.ppermute(sent, "section", across)

    saved = forward(start, ((0,), (2,)), w_up, w_down)
    gathered, picks = start, (1, 3)
    flows, added, factors, mirrored_factors = [], [], [], []
    for tick in range(TICKS):
        final = tick + 1 == TICKS
        parts, factor_up, factor_down = backward(
            gathered, picks, saved[tick], w_up, w_down, o_up, o_down, added
        )
        factors.append(factor_down)
        if tick == 0:
            parts, sent = lax.optimization_barrier((parts, sent))
        else:
            parts, mirrored_factors[-1] = lax.optimization_barrier((parts, mirrored_factors[-1]))
        if tick == 1:
            parts, row_up = lax.optimization_barrier((parts, row_up))
            mirrored = gathered_rows(jnp.concatenate([sent, row_up[None]], axis=0))
        parts = exchanged(parts)
        y_up, y_down = layer_back(
            parts,
            (x_up, flow_up, ascending_loss_gradient),
            (x_down, flow_down, descending_loss_gradient),
            tick,
            None if final else (last, 0),
        )
        if not final:
            flow_up = lax.ppermute(y_up, "section", upper)
            flow_down = lax.ppermute(y_down, "section", lower)
            gathered = repeat(flow_up, flow_down)
            gathered, row_up = lax.optimization_barrier((gathered, flow_up))
            gathered = exchanged(gathered)
            picks = (0, 1)
            flows.append(gathered)
            if tick == 0:
                saved += forward(later, ((2, 3), (0, 1)), w_up, w_down)
                gathered, row_up, factor_up, saved[1:] = lax.optimization_barrier(
                    (gathered, row_up, factor_up, saved[1:])
                )
                row_up = lax.ppermute(row_up, "section", across)
            else:
                row_up = lax.ppermute(row_up, "section", across)
                gathered, factor_up, row_up = lax.optimization_barrier((gathered, factor_up, row_up))
                added = [row_up]
        mirrored_factors.append(lax.ppermute(factor_up, "section", across))
    factors += mirrored_factors
    grad_qkv, grad_out = gradients(start, later, mirrored, flows, parts, factors)
    return (
        jnp.transpose(grad_qkv, (1, 0, 2))[None],
        grad_out[None],
        y_down[None],
        y_up[None],
    )


def solution(mesh):
    in_specs = (
        P("section", None, None, "tp"),
        P("section", "tp", None),
        P("section", None, None, "tp"),
        P("section", "tp", None),
        P("section", None, "tp", None),
        P("section", None, "tp", None),
        P("section", "tp", None),
        P("section", "tp", None),
        P(None, "tp", None),
        P(None, "tp", None),
    )
    out_specs = (
        P("section", None, None, "tp"),
        P("section", "tp", None),
        P("section", "tp", None),
        P("section", "tp", None),
    )
    return jax.shard_map(
        per_device, mesh=mesh, in_specs=in_specs, out_specs=out_specs, check_vma=False
    )
```

time: 317 us -> 272 us (0.86)
  starting transfers between devices: 132 us -> 56 us
  blocking collectives: 21.5 us -> 82.6 us
  local copies, waits for them, and re-layouts: 51.7 us -> 3.62 us
  Pallas kernels: 49.3 us -> 65.3 us
    all_to_all x1 -> x3, blocking collectives: 21.5 us -> 82.6 us  [exchanged(): return lax.all_to_all(parts, 'tp', split_axis=0, concat_axis=0, tiled=True)]
    all_to_all x8 -> x0, starting transfers between devices: 37 us -> none  [spread(): lax.all_to_all(jnp.broadcast_to(rows[None], (count,) + rows.shape), 'tp',...]
    unnamed x120 -> x34, local copies, waits for them, and re-layouts: 39.1 us -> 3.62 us
    all_to_all x6 -> x3, waiting for transfers between devices: 3.87 us -> 28.4 us  [exchanged(): return lax.all_to_all(parts, 'tp', split_axis=0, concat_axis=0, tiled=True)]
    ppermute x3, starting transfers between devices: 34.5 us -> 17 us  [the longest x1 10.1 us: per_device(): sent = lax.ppermute(sent, 'section', across)]
    all_to_all x6 -> x3, starting transfers between devices: 28.5 us -> 11 us  [exchanged(): return lax.all_to_all(parts, 'tp', split_axis=0, concat_axis=0, tiled=True)]
    all_to_all x8 -> x0, waiting for transfers between devices: 15.5 us -> none  [spread(): lax.all_to_all(jnp.broadcast_to(rows[None], (count,) + rows.shape), 'tp',...]
    pallas_call x17 -> x11, Pallas kernels: 40.2 us -> 55.5 us  [local_call(): pl.pallas_call(body, out_shape=out_shape, in_specs=in_specs or [VMEM] * l...]
  transfers between devices with their start and end apart: 26 -> 15, of which waited for: 13 -> 11; matrix products, arithmetic and copies ran while one was open for 4% -> 0% of each run, Pallas kernels for 15% -> 19%
where the time goes in v1:
time: 272 us; the launch traced here: 269 us
  blocking collectives  82.6 us (30%)
  Pallas kernels  65.3 us (24%)
  starting transfers between devices  56 us (21%)
  waiting for transfers between devices  46.5 us (17%)
  between operations  14.2 us (5%)
  local copies, waits for them, and re-layouts  3.62 us (1%)
    all_to_all x3, blocking collectives, exchanged(): return lax.all_to_all(parts, 'tp', split_axis=0, concat_axis=0, tiled=True)  82.6 us
    pallas_call x11, Pallas kernels, local_call(): pl.pallas_call(body, out_shape=out_shape, in_specs=in_specs or [VMEM] * l...  55.5 us
    all_to_all x3, waiting for transfers between devices, exchanged(): return lax.all_to_all(parts, 'tp', split_axis=0, concat_axis=0, tiled=True)  28.4 us
    ppermute x3, starting transfers between devices, per_device(): mirrored_factors.append(lax.ppermute(factor_up, 'section', across))  21.3 us
    all_to_all x3, starting transfers between devices, exchanged(): return lax.all_to_all(parts, 'tp', split_axis=0, concat_axis=0, tiled=True)  11 us
    ppermute x1, starting transfers between devices, per_device(): sent = lax.ppermute(sent, 'section', across)  10.1 us
    pallas_call x1, Pallas kernels, gradients(): pl.pallas_call(gradients_body, grid=(features // tile,), out_shape=[jax.S...  9.78 us
    ppermute x3, waiting for transfers between devices, per_device(): mirrored_factors.append(lax.ppermute(factor_up, 'section', across))  8.18 us
  transfers between devices with their start and end apart: 15, of which 11 were waited for; matrix products, arithmetic and copies ran while one was open for 0% of the time, Pallas kernels for 19%

profile of v1, /device:TPU:1, one launch (start us, length us, event | category | flops | bytes accessed | tf_op | source)
XLA Modules:
  0.0 269.0 jit_solution(17996806759463628310)
XLA Ops:
  7.2 3.5 %shard_map.129 = (bf16[8,4,16,2048]{3,2,1,0:T(8,128)(2,1)}, bf16[4,16,2048]{2,1,0:T(8,128)(2,1)}, bf16[4,16,2048]{2,1,0:T(8,128)(2,1)}) custom-call(bf16[3,16,2048]{2,1,0:T(8,128)(2,1)} %bitcast.39, bf16[3,16,2048]{2,1,0:T(8,128)(2,1)} %bitcast.43, bf16[16,2048]{1,0:T(8,128)(2,1)} %bitcast.48, bf16[16,2048]{1,0:T(8,128)(2,1)} %bitcast.50), custom_call_target="tpu_custom_call" | custom-call | flops 3932 | bytes 983 | tf_op jit(solution)/shard_map/pallas_call | solution.py:39
  10.7 31.8 %all_to_all.30.h_hbm.g_hbm.start = bf16[8,4,16,2048]{3,2,1,0:T(8,128)(2,1)} all-to-all(bf16[8,4,16,2048]{3,2,1,0:T(8,128)(2,1)} %get-tuple-element.55), channel_id=1, replica_groups=mesh['section'=32,'tp'=8] {'tp'}, dimensions={0} | all-to-all | bytes 4194304 | tf_op jit(solution)/shard_map/all_to_all | solution.py:401
  42.5 10.1 %collective-permute-start = (bf16[4,16,2048]{2,1,0:T(8,128)(2,1)S(1)}, bf16[4,16,2048]{2,1,0:T(8,128)(2,1)S(1)}, u32[]{:S(2)}, u32[]{:S(2)}) collective-permute-start(bf16[4,16,2048]{2,1,0:T(8,128)(2,1)S(1)} %copy-done.16), channel_id=1, source_target_pairs={{0,248},{8,240},{16,232},{24,224},{32,216},{40,208},{48,200},{56,1... | collective-permute-start | bytes 786440 | tf_op jit(solution)/shard_map/ppermute | solution.py:439
  52.6 5.7 %shard_map.130 = (bf16[2,4,128,256]{3,2,1,0:T(8,128)(2,1)}, f32[2,2,128,128]{3,2,1,0:T(8,128)}) custom-call(bf16[8,4,16,2048]{3,2,1,0:T(8,128)(2,1)} %all_to_all.30.h_hbm.g_hbm.start, bf16[3,2048,256]{2,1,0:T(8,128)(2,1)} %bitcast.21, bf16[3,2048,256]{2,1,0:T(8,128)(2,1)} %bitcast.26), custom_call_target="tpu_custom_call" | custom-call | flops 805306 | bytes 8388 | tf_op jit(solution)/shard_map/pallas_call | solution.py:39
  58.4 8.2 %shard_map.131 = (bf16[8,2,16,2048]{3,2,1,0:T(8,128)(2,1)}, bf16[4,128,256]{2,1,0:T(8,128)(2,1)}, bf16[4,128,256]{2,1,0:T(8,128)(2,1)}) custom-call(bf16[8,4,16,2048]{3,2,1,0:T(8,128)(2,1)} %all_to_all.30.h_hbm.g_hbm.start, bf16[2,4,128,256]{3,2,1,0:T(8,128)(2,1)} %get-tuple-element.60.qkv_hbm, f32[2,2,128,128]{3,2,1,0:T(8,128)} %get-tuple-element.61.soft_hbm, ...), custom_call_target="tpu_custom_call" | custom-call | flops 1073741 | bytes 12582 | tf_op jit(solution)/shard_map/pallas_call | solution.py:39
  66.5 25.5 %all_to_all.31.parts_ref = bf16[8,2,16,2048]{3,2,1,0:T(8,128)(2,1)} all-to-all(bf16[8,2,16,2048]{3,2,1,0:T(8,128)(2,1)} %get-tuple-element.65), channel_id=1, replica_groups=mesh['section'=32,'tp'=8] {'tp'}, dimensions={0} | all-to-all | bytes 2097152 | tf_op jit(solution)/shard_map/all_to_all | solution.py:401
  92.1 2.6 shard_map.132
  94.6 2.0 collective-permute-start.1
  98.3 2.5 collective-permute-done.2.refs_1_.refs_4_
  101.5 2.0 shard_map.133
  103.4 3.6 %all-to-all-start.2 = ((bf16[8,2,16,2048]{3,2,1,0:T(8,128)(2,1)}), bf16[8,2,16,2048]{3,2,1,0:T(8,128)(2,1)S(1)}, u32[]{:S(2)}, u32[]{:S(2)}) async-start(bf16[8,2,16,2048]{3,2,1,0:T(8,128)(2,1)} %shard_map.133), calls=%async_computation.2 | async-start | bytes 2097152 | tf_op jit(solution)/shard_map/all_to_all | solution.py:401
  107.1 9.0 %shard_map.134 = (bf16[2,4,128,256]{3,2,1,0:T(8,128)(2,1)}, f32[2,2,128,128]{3,2,1,0:T(8,128)}, bf16[2,4,128,256]{3,2,1,0:T(8,128)(2,1)}, f32[2,2,128,128]{3,2,1,0:T(8,128)}) custom-call(bf16[8,4,16,2048]{3,2,1,0:T(8,128)(2,1)} %bitcast.37, bf16[3,2048,256]{2,1,0:T(8,128)(2,1)} %bitcast.23, bf16[3,2048,256]{2,1,0:T(8,128)(2,1)} %bitcast.28), custom_call_target="tpu_custom_call" | custom-call | flops 1610612 | bytes 8388 | tf_op jit(solution)/shard_map/pallas_call | solution.py:39
  116.1 2.0 all-to-all-done.2.g_hbm.g1
  118.1 11.7 %collective-permute-start.3 = (bf16[4,128,256]{2,1,0:T(8,128)(2,1)S(1)}, bf16[4,128,256]{2,1,0:T(8,128)(2,1)S(1)}, u32[]{:S(2)}, u32[]{:S(2)}) collective-permute-start(bf16[4,128,256]{2,1,0:T(8,128)(2,1)S(1)} %copy-done.14), channel_id=1, source_target_pairs={{0,248},{8,240},{16,232},{24,224},{32,216},{40,208},{48,200},{56,1... | collective-permute-start | bytes 786440 | tf_op jit(solution)/shard_map/ppermute | solution.py:483
  130.1 8.2 %shard_map.135 = (bf16[8,2,16,2048]{3,2,1,0:T(8,128)(2,1)}, bf16[4,128,256]{2,1,0:T(8,128)(2,1)}, bf16[4,128,256]{2,1,0:T(8,128)(2,1)}) custom-call(bf16[8,2,16,2048]{3,2,1,0:T(8,128)(2,1)} %copy-done.1, bf16[2,4,128,256]{3,2,1,0:T(8,128)(2,1)} %get-tuple-element.76.qkv_hbm, f32[2,2,128,128]{3,2,1,0:T(8,128)} %get-tuple-element.77.soft_hbm, ...), custom_call_target="tpu_custom_call" | custom-call | flops 1073741 | bytes 12582 | tf_op jit(solution)/shard_map/pallas_call | solution.py:39
  138.2 5.6 %collective-permute-done.3.rest_3_ = bf16[4,128,256]{2,1,0:T(8,128)(2,1)S(1)} collective-permute-done((bf16[4,128,256]{2,1,0:T(8,128)(2,1)S(1)}, bf16[4,128,256]{2,1,0:T(8,128)(2,1)S(1)}, u32[]{:S(2)}, u32[]{:S(2)}) %collective-permute-start.3) | collective-permute-done | bytes 262176 | tf_op jit(solution)/shard_map/ppermute | solution.py:483
  145.5 25.3 %all_to_all.32.parts_ref = bf16[8,2,16,2048]{3,2,1,0:T(8,128)(2,1)} all-to-all(bf16[8,2,16,2048]{3,2,1,0:T(8,128)(2,1)} %get-tuple-element.83), channel_id=1, replica_groups=mesh['section'=32,'tp'=8] {'tp'}, dimensions={0} | all-to-all | bytes 2097152 | tf_op jit(solution)/shard_map/all_to_all | solution.py:401
  170.7 2.6 shard_map.136
  173.4 4.5 %collective-permute-start.6 = (bf16[16,2048]{1,0:T(8,128)(2,1)}, bf16[16,2048]{1,0:T(8,128)(2,1)S(1)}, u32[]{:S(2)}, u32[]{:S(2)}) collective-permute-start(bf16[16,2048]{1,0:T(8,128)(2,1)} %get-tuple-element.85), channel_id=1, source_target_pairs={{0,248},{8,0},{16,8},{24,16},{32,24},{40,32},{48,40},{56,48},{64,5... | collective-permute-start | bytes 196616 | tf_op jit(solution)/shard_map/ppermute | solution.py:467
  180.0 2.0 shard_map.137
  182.0 3.7 %all-to-all-start.4 = ((bf16[8,2,16,2048]{3,2,1,0:T(8,128)(2,1)}), bf16[8,2,16,2048]{3,2,1,0:T(8,128)(2,1)S(1)}, u32[]{:S(2)}, u32[]{:S(2)}) async-start(bf16[8,2,16,2048]{3,2,1,0:T(8,128)(2,1)} %shard_map.137), calls=%async_computation.4 | async-start | bytes 2097152 | tf_op jit(solution)/shard_map/all_to_all | solution.py:401
  185.7 6.7 %collective-permute-start.7 = (bf16[16,2048]{1,0:T(8,128)(2,1)S(1)}, bf16[16,2048]{1,0:T(8,128)(2,1)S(1)}, u32[]{:S(2)}, u32[]{:S(2)}) collective-permute-start(bf16[16,2048]{1,0:T(8,128)(2,1)S(1)} %copy-done.10), channel_id=1, source_target_pairs={{0,248},{8,240},{16,232},{24,224},{32,216},{40,208},{48,200},{56,1... | collective-permute-start | bytes 196616 | tf_op jit(solution)/shard_map/ppermute | solution.py:480
  192.4 3.8 %collective-permute-done.7.rest_0_ = bf16[16,2048]{1,0:T(8,128)(2,1)S(1)} collective-permute-done((bf16[16,2048]{1,0:T(8,128)(2,1)S(1)}, bf16[16,2048]{1,0:T(8,128)(2,1)S(1)}, u32[]{:S(2)}, u32[]{:S(2)}) %collective-permute-start.7) | collective-permute-done | bytes 65568 | tf_op jit(solution)/shard_map/ppermute | solution.py:480
  196.1 8.3 %all-to-all-done.4.g_hbm.g2 = bf16[8,2,16,2048]{3,2,1,0:T(8,128)(2,1)S(1)} async-done(((bf16[8,2,16,2048]{3,2,1,0:T(8,128)(2,1)}), bf16[8,2,16,2048]{3,2,1,0:T(8,128)(2,1)S(1)}, u32[]{:S(2)}, u32[]{:S(2)}) %all-to-all-start.4) | async-done | bytes 1048608 | tf_op jit(solution)/shard_map/all_to_all | solution.py:401
  204.4 3.1 %collective-permute-start.8 = (bf16[4,128,256]{2,1,0:T(8,128)(2,1)S(1)}, bf16[4,128,256]{2,1,0:T(8,128)(2,1)S(1)}, u32[]{:S(2)}, u32[]{:S(2)}) collective-permute-start(bf16[4,128,256]{2,1,0:T(8,128)(2,1)S(1)} %copy-done.13), channel_id=1, source_target_pairs={{0,248},{8,240},{16,232},{24,224},{32,216},{40,208},{48,200},{56,1... | collective-permute-start | bytes 786440 | tf_op jit(solution)/shard_map/ppermute | solution.py:483
  207.6 9.2 %shard_map.138 = (bf16[8,3,16,2048]{3,2,1,0:T(8,128)(2,1)}, bf16[4,128,256]{2,1,0:T(8,128)(2,1)}, bf16[4,128,256]{2,1,0:T(8,128)(2,1)}) custom-call(bf16[8,2,16,2048]{3,2,1,0:T(8,128)(2,1)} %copy-done.2, bf16[2,4,128,256]{3,2,1,0:T(8,128)(2,1)} %get-tuple-element.90.qkv_hbm, f32[2,2,128,128]{3,2,1,0:T(8,128)} %get-tuple-element.91.soft_hbm, ...), custom_call_target="tpu_custom_call" | custom-call | flops 1073741 | bytes 12582 | tf_op jit(solution)/shard_map/pallas_call | solution.py:39
  216.8 2.5 collective-permute-done.8.rest_4_
  219.3 3.8 %all-to-all-start.5 = ((bf16[8,3,16,2048]{3,2,1,0:T(8,128)(2,1)}), bf16[8,3,16,2048]{3,2,1,0:T(8,128)(2,1)S(1)}, u32[]{:S(2)}, u32[]{:S(2)}) async-start(bf16[8,3,16,2048]{3,2,1,0:T(8,128)(2,1)} %get-tuple-element.95), calls=%async_computation.5 | async-start | bytes 3145728 | tf_op jit(solution)/shard_map/all_to_all | solution.py:401
  223.1 6.5 %collective-permute-start.9 = (bf16[4,128,256]{2,1,0:T(8,128)(2,1)S(1)}, bf16[4,128,256]{2,1,0:T(8,128)(2,1)S(1)}, u32[]{:S(2)}, u32[]{:S(2)}) collective-permute-start(bf16[4,128,256]{2,1,0:T(8,128)(2,1)S(1)} %copy-done.15), channel_id=1, source_target_pairs={{0,248},{8,240},{16,232},{24,224},{32,216},{40,208},{48,200},{56,1... | collective-permute-start | bytes 786440 | tf_op jit(solution)/shard_map/ppermute | solution.py:483
  229.5 18.2 %all-to-all-done.5.moved.parts_ref = bf16[8,3,16,2048]{3,2,1,0:T(8,128)(2,1)S(1)} async-done(((bf16[8,3,16,2048]{3,2,1,0:T(8,128)(2,1)}), bf16[8,3,16,2048]{3,2,1,0:T(8,128)(2,1)S(1)}, u32[]{:S(2)}, u32[]{:S(2)}) %all-to-all-start.5) | async-done | bytes 1572896 | tf_op jit(solution)/shard_map/all_to_all | solution.py:401
  249.0 2.7 %shard_map.140 = (bf16[16,2048]{1,0:T(8,128)(2,1)}, bf16[16,2048]{1,0:T(8,128)(2,1)}) custom-call(bf16[8,3,16,2048]{3,2,1,0:T(8,128)(2,1)} %copy-done, bf16[3,16,2048]{2,1,0:T(8,128)(2,1)} %bitcast.46, bf16[16,2048]{1,0:T(8,128)(2,1)} %copy-done.9, bf16[2,16,2048]{2,1,0:T(8,128)(2,1)} %refs_2_.5, bf16[3,16,2048]{2,1,0:T(8,128)(2,1)} %bitcast.42, ...), custom_call_target="tpu_custom_call" | custom-call | flops 15728 | bytes 2359 | tf_op jit(solution)/shard_map/pallas_call | solution.py:39
  252.4 9.8 %shard_map.139 = (bf16[3,2048,256]{2,1,0:T(8,128)(2,1)}, bf16[256,2048]{1,0:T(8,128)(2,1)}) custom-call(bf16[8,4,16,2048]{3,2,1,0:T(8,128)(2,1)} %all_to_all.30.h_hbm.g_hbm.start, bf16[8,4,16,2048]{3,2,1,0:T(8,128)(2,1)} %bitcast.38, bf16[8,5,16,2048]{3,2,1,0:T(8,128)(2,1)} %bitcast.47, bf16[8,2,16,2048]{3,2,1,0:T(8,128)(2,1)} %copy-done.1, ...), custom_call_target="tpu_custom_call" | custom-call | flops 3221225472 | bytes 12582912 | tf_op jit(solution)/shard_map/pallas_call | solution.py:373
  (50 shorter events, 8.4 us)
Async XLA Ops:
  7.2 99.9 %all-gather.5.cloned.1.call-start = ((), (), s32[]{:S(2)}) async-start(), calls=%async_computation.6 | async-start | bytes 2359296 | tf_op jit(solution)/shard_map/all_gather | solution.py:405
  10.7 31.8 %copy-start.16 = (bf16[4,16,2048]{2,1,0:T(8,128)(2,1)S(1)}, bf16[4,16,2048]{2,1,0:T(8,128)(2,1)}, u32[]{:S(2)}) copy-start(bf16[4,16,2048]{2,1,0:T(8,128)(2,1)} %get-tuple-element.63) | copy-start | bytes 786436
  42.5 24.0 %collective-permute-start = (bf16[4,16,2048]{2,1,0:T(8,128)(2,1)S(1)}, bf16[4,16,2048]{2,1,0:T(8,128)(2,1)S(1)}, u32[]{:S(2)}, u32[]{:S(2)}) collective-permute-start(bf16[4,16,2048]{2,1,0:T(8,128)(2,1)S(1)} %copy-done.16), channel_id=1, source_target_pairs={{0,248},{8,240},{16,232},{24,224},{32,216},{40,208},{48,200},{56,1... | collective-permute-start | bytes 786440 | tf_op jit(solution)/shard_map/ppermute | solution.py:439
  94.6 3.7 %collective-permute-start.1 = (bf16[16,2048]{1,0:T(8,128)(2,1)}, bf16[16,2048]{1,0:T(8,128)(2,1)S(1)}, u32[]{:S(2)}, u32[]{:S(2)}) collective-permute-start(bf16[16,2048]{1,0:T(8,128)(2,1)} %get-tuple-element.66), channel_id=1, source_target_pairs={{0,8},{8,16},{16,24},{24,32},{32,40},{40,48},{48,56},{56,64},{64,7... | collective-permute-start | bytes 196616 | tf_op jit(solution)/shard_map/ppermute | solution.py:466
  96.6 4.2 %collective-permute-start.2 = (bf16[16,2048]{1,0:T(8,128)(2,1)}, bf16[16,2048]{1,0:T(8,128)(2,1)S(1)}, u32[]{:S(2)}, u32[]{:S(2)}) collective-permute-start(bf16[16,2048]{1,0:T(8,128)(2,1)} %get-tuple-element.67), channel_id=1, source_target_pairs={{0,248},{8,0},{16,8},{24,16},{32,24},{40,32},{48,40},{56,48},{64,5... | collective-permute-start | bytes 196616 | tf_op jit(solution)/shard_map/ppermute | solution.py:467
  98.3 2.6 copy-start.6
  100.8 0.6 copy-start.8
  103.4 14.7 %all-to-all-start.2 = ((bf16[8,2,16,2048]{3,2,1,0:T(8,128)(2,1)}), bf16[8,2,16,2048]{3,2,1,0:T(8,128)(2,1)S(1)}, u32[]{:S(2)}, u32[]{:S(2)}) async-start(bf16[8,2,16,2048]{3,2,1,0:T(8,128)(2,1)} %shard_map.133), calls=%async_computation.2 | async-start | bytes 2097152 | tf_op jit(solution)/shard_map/all_to_all | solution.py:401
  107.0 144.7 %all-gather.7.cloned.1.call-start = ((), (), s32[]{:S(2)}) async-start(), calls=%async_computation.7 | async-start | bytes 2949120 | tf_op jit(solution)/shard_map/all_gather | solution.py:405
  107.1 11.0 %copy-start.14 = (bf16[4,128,256]{2,1,0:T(8,128)(2,1)S(1)}, bf16[4,128,256]{2,1,0:T(8,128)(2,1)}, u32[]{:S(2)}) copy-start(bf16[4,128,256]{2,1,0:T(8,128)(2,1)} %get-tuple-element.79) | copy-start | bytes 786436
  107.1 22.7 %copy-start.7 = (bf16[16,2048]{1,0:T(8,128)(2,1)S(1)}, bf16[16,2048]{1,0:T(8,128)(2,1)}, u32[]{:S(2)}) copy-start(bf16[16,2048]{1,0:T(8,128)(2,1)} %copy-done.6) | copy-start | bytes 196612
  118.1 12.0 %copy-start.1 = (bf16[8,2,16,2048]{3,2,1,0:T(8,128)(2,1)}, bf16[8,2,16,2048]{3,2,1,0:T(8,128)(2,1)S(1)}, u32[]{:S(2)}) copy-start(bf16[8,2,16,2048]{3,2,1,0:T(8,128)(2,1)S(1)} %all-to-all-done.2.g_hbm.g1) | copy-start | bytes 3145732
  118.1 25.8 %collective-permute-start.3 = (bf16[4,128,256]{2,1,0:T(8,128)(2,1)S(1)}, bf16[4,128,256]{2,1,0:T(8,128)(2,1)S(1)}, u32[]{:S(2)}, u32[]{:S(2)}) collective-permute-start(bf16[4,128,256]{2,1,0:T(8,128)(2,1)S(1)} %copy-done.14), channel_id=1, source_target_pairs={{0,248},{8,240},{16,232},{24,224},{32,216},{40,208},{48,200},{56,1... | collective-permute-start | bytes 786440 | tf_op jit(solution)/shard_map/ppermute | solution.py:483
  129.8 14.9 %collective-permute-start.4 = (bf16[16,2048]{1,0:T(8,128)(2,1)S(1)}, bf16[16,2048]{1,0:T(8,128)(2,1)S(1)}, u32[]{:S(2)}, u32[]{:S(2)}) collective-permute-start(bf16[16,2048]{1,0:T(8,128)(2,1)S(1)} %copy-done.7), channel_id=1, source_target_pairs={{0,248},{8,240},{16,232},{24,224},{32,216},{40,208},{48,200},{56,1... | collective-permute-start | bytes 196616 | tf_op jit(solution)/shard_map/ppermute | solution.py:478
  143.9 29.4 %copy-start.3 = (bf16[4,128,256]{2,1,0:T(8,128)(2,1)}, bf16[4,128,256]{2,1,0:T(8,128)(2,1)S(1)}, u32[]{:S(2)}) copy-start(bf16[4,128,256]{2,1,0:T(8,128)(2,1)S(1)} %collective-permute-done.3.rest_3_) | copy-start | bytes 786436
  173.3 31.1 %copy-start.13 = (bf16[4,128,256]{2,1,0:T(8,128)(2,1)S(1)}, bf16[4,128,256]{2,1,0:T(8,128)(2,1)}, u32[]{:S(2)}) copy-start(bf16[4,128,256]{2,1,0:T(8,128)(2,1)} %get-tuple-element.94) | copy-start | bytes 786436
  173.3 5.4 %collective-permute-start.5 = (bf16[16,2048]{1,0:T(8,128)(2,1)}, bf16[16,2048]{1,0:T(8,128)(2,1)S(1)}, u32[]{:S(2)}, u32[]{:S(2)}) collective-permute-start(bf16[16,2048]{1,0:T(8,128)(2,1)} %get-tuple-element.84), channel_id=1, source_target_pairs={{0,8},{8,16},{16,24},{24,32},{32,40},{40,48},{48,56},{56,64},{64,7... | collective-permute-start | bytes 196616 | tf_op jit(solution)/shard_map/ppermute | solution.py:466
  173.4 5.6 %collective-permute-start.6 = (bf16[16,2048]{1,0:T(8,128)(2,1)}, bf16[16,2048]{1,0:T(8,128)(2,1)S(1)}, u32[]{:S(2)}, u32[]{:S(2)}) collective-permute-start(bf16[16,2048]{1,0:T(8,128)(2,1)} %get-tuple-element.85), channel_id=1, source_target_pairs={{0,248},{8,0},{16,8},{24,16},{32,24},{40,32},{48,40},{56,48},{64,5... | collective-permute-start | bytes 196616 | tf_op jit(solution)/shard_map/ppermute | solution.py:467
  178.7 0.6 copy-start.9
  179.4 0.6 copy-start.11
  182.0 3.7 %copy-start.10 = (bf16[16,2048]{1,0:T(8,128)(2,1)S(1)}, bf16[16,2048]{1,0:T(8,128)(2,1)}, u32[]{:S(2)}) copy-start(bf16[16,2048]{1,0:T(8,128)(2,1)} %copy-done.9) | copy-start | bytes 196612
  182.0 22.4 %all-to-all-start.4 = ((bf16[8,2,16,2048]{3,2,1,0:T(8,128)(2,1)}), bf16[8,2,16,2048]{3,2,1,0:T(8,128)(2,1)S(1)}, u32[]{:S(2)}, u32[]{:S(2)}) async-start(bf16[8,2,16,2048]{3,2,1,0:T(8,128)(2,1)} %shard_map.137), calls=%async_computation.4 | async-start | bytes 2097152 | tf_op jit(solution)/shard_map/all_to_all | solution.py:401
  185.7 10.4 %collective-permute-start.7 = (bf16[16,2048]{1,0:T(8,128)(2,1)S(1)}, bf16[16,2048]{1,0:T(8,128)(2,1)S(1)}, u32[]{:S(2)}, u32[]{:S(2)}) collective-permute-start(bf16[16,2048]{1,0:T(8,128)(2,1)S(1)} %copy-done.10), channel_id=1, source_target_pairs={{0,248},{8,240},{16,232},{24,224},{32,216},{40,208},{48,200},{56,1... | collective-permute-start | bytes 196616 | tf_op jit(solution)/shard_map/ppermute | solution.py:480
  196.1 11.4 %copy-start.12 = (bf16[16,2048]{1,0:T(8,128)(2,1)}, bf16[16,2048]{1,0:T(8,128)(2,1)S(1)}, u32[]{:S(2)}) copy-start(bf16[16,2048]{1,0:T(8,128)(2,1)S(1)} %collective-permute-done.7.rest_0_) | copy-start | bytes 196612
  204.4 3.2 %copy-start.2 = (bf16[8,2,16,2048]{3,2,1,0:T(8,128)(2,1)}, bf16[8,2,16,2048]{3,2,1,0:T(8,128)(2,1)S(1)}, u32[]{:S(2)}) copy-start(bf16[8,2,16,2048]{3,2,1,0:T(8,128)(2,1)S(1)} %all-to-all-done.4.g_hbm.g2) | copy-start | bytes 3145732
  204.4 14.9 %collective-permute-start.8 = (bf16[4,128,256]{2,1,0:T(8,128)(2,1)S(1)}, bf16[4,128,256]{2,1,0:T(8,128)(2,1)S(1)}, u32[]{:S(2)}, u32[]{:S(2)}) collective-permute-start(bf16[4,128,256]{2,1,0:T(8,128)(2,1)S(1)} %copy-done.13), channel_id=1, source_target_pairs={{0,248},{8,240},{16,232},{24,224},{32,216},{40,208},{48,200},{56,1... | collective-permute-start | bytes 786440 | tf_op jit(solution)/shard_map/ppermute | solution.py:483
  216.8 6.3 %copy-start.15 = (bf16[4,128,256]{2,1,0:T(8,128)(2,1)S(1)}, bf16[4,128,256]{2,1,0:T(8,128)(2,1)}, u32[]{:S(2)}) copy-start(bf16[4,128,256]{2,1,0:T(8,128)(2,1)} %get-tuple-element.101) | copy-start | bytes 786436
  219.3 32.4 %copy-start.4 = (bf16[4,128,256]{2,1,0:T(8,128)(2,1)}, bf16[4,128,256]{2,1,0:T(8,128)(2,1)S(1)}, u32[]{:S(2)}) copy-start(bf16[4,128,256]{2,1,0:T(8,128)(2,1)S(1)} %collective-permute-done.8.rest_4_) | copy-start | bytes 786436
  219.3 28.4 %all-to-all-start.5 = ((bf16[8,3,16,2048]{3,2,1,0:T(8,128)(2,1)}), bf16[8,3,16,2048]{3,2,1,0:T(8,128)(2,1)S(1)}, u32[]{:S(2)}, u32[]{:S(2)}) async-start(bf16[8,3,16,2048]{3,2,1,0:T(8,128)(2,1)} %get-tuple-element.95), calls=%async_computation.5 | async-start | bytes 3145728 | tf_op jit(solution)/shard_map/all_to_all | solution.py:401
  223.1 28.6 %collective-permute-start.9 = (bf16[4,128,256]{2,1,0:T(8,128)(2,1)S(1)}, bf16[4,128,256]{2,1,0:T(8,128)(2,1)S(1)}, u32[]{:S(2)}, u32[]{:S(2)}) collective-permute-start(bf16[4,128,256]{2,1,0:T(8,128)(2,1)S(1)} %copy-done.15), channel_id=1, source_target_pairs={{0,248},{8,240},{16,232},{24,224},{32,216},{40,208},{48,200},{56,1... | collective-permute-start | bytes 786440 | tf_op jit(solution)/shard_map/ppermute | solution.py:483
  247.7 1.2 copy-start
  251.7 0.7 copy-start.5
Sparse Core Ops, SparseCore 0:
  42.6 51.9 all-gather.4
  145.6 47.0 all-gather.6

commit v2 on v1

--- a/solution.py
+++ b/solution.py
@@ -142,30 +142,39 @@
     causal = lax.broadcasted_iota(jnp.int32, (rows, rows), 0) >= lax.broadcasted_iota(
         jnp.int32, (rows, rows), 1
     )
+    projected = []
     for pipe in range(2):
         for copy in h_copies[pipe]:
             copy.wait()
         hidden = h_all[pipe].reshape(count * rows, features)
-        projected = []
         for part in range(3):
             w_copies[pipe][part].wait()
             projected.append(dot_nn(hidden, w_all[pipe, part]).astype(jnp.bfloat16))
-        queries, keys, values = projected
+    places = [
+        (pipe, index, head, slice(index * rows, (index + 1) * rows), slice(head * HEAD, (head + 1) * HEAD))
+        for pipe in range(2)
+        for index in range(count)
+        for head in range(local // HEAD)
+    ]
+    scores = [
+        dot_nt(projected[3 * pipe][span, cols], projected[3 * pipe + 1][span, cols])
+        for pipe, _, _, span, cols in places
+    ]
+    scores = [jnp.where(causal, score * HEAD ** (-0.5), -jnp.inf) for score in scores]
+    powers = [jnp.exp(score - jnp.max(score, axis=-1, keepdims=True)) for score in scores]
+    softs = [power / jnp.sum(power, axis=-1, keepdims=True) for power in powers]
+    mixed = [
+        dot_nn(soft.astype(jnp.bfloat16), projected[3 * pipe + 2][span, cols]).astype(jnp.bfloat16)
+        for soft, (pipe, _, _, span, cols) in zip(softs, places)
+    ]
+    for pipe in range(2):
         for index in range(count):
-            qkv_ref, soft_ref = outs[2 * index : 2 * index + 2]
             span = slice(index * rows, (index + 1) * rows)
             for part in range(3):
-                qkv_ref[pipe, part] = projected[part][span]
-            for head in range(local // HEAD):
-                cols = slice(head * HEAD, (head + 1) * HEAD)
-                scores = dot_nt(queries[span, cols], keys[span, cols]) * HEAD ** (-0.5)
-                scores = jnp.where(causal, scores, -jnp.inf)
-                powers = jnp.exp(scores - jnp.max(scores, axis=-1, keepdims=True))
-                soft = powers / jnp.sum(powers, axis=-1, keepdims=True)
-                soft_ref[pipe, head] = soft
-                qkv_ref[pipe, 3, :, cols] = dot_nn(
-                    soft.astype(jnp.bfloat16), values[span, cols]
-                ).astype(jnp.bfloat16)
+                outs[2 * index][pipe, part] = projected[3 * pipe + part][span]
+    for soft, mix, (pipe, index, head, _, cols) in zip(softs, mixed, places):
+        outs[2 * index + 1][pipe, head] = soft
+        outs[2 * index][pipe, 3, :, cols] = mix
 
 
 def forward(hidden, picks, w_up, w_down):
@@ -200,7 +209,7 @@
     shards, shard_rows, features = g_all.shape[1:]
     rows = shards * shard_rows
     local = o_all.shape[1]
-    tile = 512
+    tile = 1024
     copy = pltpu.make_async_copy
     first, second = [], []
     for pipe in range(2):
@@ -212,7 +221,7 @@
                 copy(soft_hbm.at[pipe], soft_all.at[pipe], sem.at[pipe, 3]),
             ]
         )
-        second.append([copy((w_up, w_down)[pipe], w_all.at[pipe], sem.at[pipe, 4])])
+        second.append([copy((w_up, w_down)[pipe].at[part, pl.ds(half * 1024, 1024)], w_all.at[pipe, part, pl.ds(half * 1024, 1024)], sem.at[pipe, 4 + 2 * part + half]) for part in range(3) for half in range(2)])
     for group in first + second:
         for one in group:
             one.start()
@@ -224,31 +233,33 @@
     ]
     for one in sent:
         one.start()
+    arrived = []
     for pipe in range(2):
         for one in first[pipe]:
             one.wait()
         upstream = g_all[pipe].reshape(rows, features)
-        d_attended = dot_nt(upstream, o_all[pipe]).astype(jnp.bfloat16)
-        d_queries, d_keys, d_values = [], [], []
-        for head in range(local // HEAD):
-            cols = slice(head * HEAD, (head + 1) * HEAD)
-            queries, keys, values, attended = [qkv[pipe, part, :, cols] for part in range(4)]
-            soft = soft_all[pipe, head]
-            d_here = d_attended[:, cols]
-            d_values.append(dot_tn(soft.astype(jnp.bfloat16), d_here).astype(jnp.bfloat16))
-            d_probs = dot_nt(d_here, values)
-            offset = jnp.sum(
-                d_here.astype(jnp.float32) * attended.astype(jnp.float32), axis=-1, keepdims=True
-            )
-            d_scores = (soft * (d_probs - offset) * HEAD ** (-0.5)).astype(jnp.bfloat16)
-            d_queries.append(dot_nn(d_scores, keys).astype(jnp.bfloat16))
-            d_keys.append(dot_tn(d_scores, queries).astype(jnp.bfloat16))
-        pieces.append([jnp.concatenate(parts, axis=1) for parts in (d_queries, d_keys, d_values)])
-        for part in range(3):
-            factor[pipe, part] = pieces[pipe][part]
+        arrived.append(dot_nt(upstream, o_all[pipe]).astype(jnp.bfloat16))
+    heads = [(pipe, head, slice(head * HEAD, (head + 1) * HEAD)) for pipe in range(2) for head in range(local // HEAD)]
+    here = [arrived[pipe][:, cols] for pipe, _, cols in heads]
+    d_probs = [dot_nt(d_here, qkv[pipe, 2, :, cols]) for d_here, (pipe, _, cols) in zip(here, heads)]
+    offsets = [
+        jnp.sum(d_here.astype(jnp.float32) * qkv[pipe, 3, :, cols].astype(jnp.float32), axis=-1, keepdims=True)
+        for d_here, (pipe, _, cols) in zip(here, heads)
+    ]
+    softs = [soft_all[pipe, head] for pipe, head, _ in heads]
+    d_scores = [
+        (soft * (d_prob - offset) * HEAD ** (-0.5)).astype(jnp.bfloat16)
+        for soft, d_prob, offset in zip(softs, d_probs, offsets)
+    ]
+    for soft, d_here, d_score, (pipe, _, cols) in zip(softs, here, d_scores, heads):
+        factor[pipe, 0, :, cols] = dot_nn(d_score, qkv[pipe, 1, :, cols]).astype(jnp.bfloat16)
+        factor[pipe, 1, :, cols] = dot_tn(d_score, qkv[pipe, 0, :, cols]).astype(jnp.bfloat16)
+        factor[pipe, 2, :, cols] = dot_tn(soft.astype(jnp.bfloat16), d_here).astype(jnp.bfloat16)
+    for pipe in range(2):
         factor[pipe, 3] = qkv[pipe, 3]
         sent.append(copy(factor.at[pipe], (factor_up, factor_down)[pipe], out_sem.at[pipe, 0]))
         sent[-1].start()
+    pieces = [[factor[pipe, part] for part in range(3)] for pipe in range(2)]
     for pipe in range(2):
         for one in second[pipe]:
             one.wait()
@@ -291,8 +302,8 @@
             pltpu.VMEM((2, local, features), jnp.bfloat16),
             pltpu.VMEM((2,) + wide, jnp.bfloat16),
             pltpu.VMEM((2, 4, rows, local), jnp.bfloat16),
-            pltpu.SemaphoreType.DMA((2, 5)),
-            pltpu.SemaphoreType.DMA((2, 1 + features // 512 + shards)),
+            pltpu.SemaphoreType.DMA((2, 10)),
+            pltpu.SemaphoreType.DMA((2, 1 + features // 1024 + shards)),
         ],
     )
 
@@ -326,9 +337,8 @@
     )
 
 
-def gradients_body(start, later, mirrored, g1, g2, moved, *rest):
-    factors = rest[:6]
-    w_ref, o_ref, d_all, a_all = rest[6:]
+def qkv_gradient_body(start, later, mirrored, *rest):
+    factors, (w_ref, d_all) = rest[:6], rest[6:]
     rows = factors[0].shape[1]
     tile = start.shape[-1]
 
@@ -337,7 +347,6 @@
         for index, factor in enumerate(factors):
             for part in range(3):
                 d_all[part, index * rows : (index + 1) * rows, :] = factor[part]
-            a_all[:, index * rows : (index + 1) * rows] = factor[3].T
 
     def flat(block):
         return block.reshape(rows, tile)
@@ -347,50 +356,82 @@
         + [flat(mirrored[:, index]) for index in range(TICKS)],
         axis=0,
     )
-    upstream = jnp.concatenate(
-        [flat(start[:, 1]), flat(g1[:, 0]), flat(g2[:, 0])]
-        + [flat(mirrored[:, TICKS]), flat(mirrored[:, TICKS + 1]), flat(moved[:, 0])],
-        axis=0,
-    )
     turned = hidden.T
     for part in range(3):
         w_ref[part] = dot_nn(turned, d_all[part]).astype(jnp.bfloat16)
-    o_ref[...] = dot_nn(a_all[...], upstream).astype(jnp.bfloat16)
-
-
-def gradients(start, later, mirrored, gathered, moved, factors):
-    features = start.shape[-1]
+
+
+def qkv_gradient(start, later, mirrored, factors):
+    shards, _, shard_rows, features = start.shape
     rows, local = factors[0].shape[1:]
     tile = 256
-    shards = start.shape[0]
-    shard_rows = start.shape[2]
 
     def columns(count, at=0):
         return pl.BlockSpec((shards, count, shard_rows, tile), lambda i: (0, at, 0, i))
 
-    whole = pl.BlockSpec((4, rows, local), lambda i: (0, 0, 0))
+    whole = pl.BlockSpec((3, rows, local), lambda i: (0, 0, 0))
     depth = 2 * TICKS * rows
     return pl.pallas_call(
-        gradients_body,
+        qkv_gradient_body,
         grid=(features // tile,),
-        out_shape=[
-            jax.ShapeDtypeStruct((3, features, local), jnp.bfloat16),
-            jax.ShapeDtypeStruct((local, features), jnp.bfloat16),
-        ],
-        in_specs=[columns(2, 1), columns(2), columns(TICKS + 2), columns(1, 1), columns(1, 1), columns(1, 2)] + [whole] * 6,
-        out_specs=[
-            pl.BlockSpec((3, tile, local), lambda i: (0, i, 0)),
-            pl.BlockSpec((local, tile), lambda i: (0, i)),
-        ],
-        scratch_shapes=[
-            pltpu.VMEM((3, depth, local), jnp.bfloat16),
-            pltpu.VMEM((local, depth), jnp.bfloat16),
-        ],
+        out_shape=jax.ShapeDtypeStruct((3, features, local), jnp.bfloat16),
+        in_specs=[columns(1, 2), columns(2), columns(TICKS)] + [whole] * 6,
+        out_specs=pl.BlockSpec((3, tile, local), lambda i: (0, i, 0)),
+        scratch_shapes=[pltpu.VMEM((3, depth, local), jnp.bfloat16)],
         compiler_params=pltpu.CompilerParams(vmem_limit_bytes=ROOM),
         cost_estimate=pl.CostEstimate(
-            flops=2 * depth * features * 4 * local, bytes_accessed=12 * MIB, transcendentals=0
+            flops=600 * depth * features * local, bytes_accessed=800 * MIB, transcendentals=0
         ),
-    )(start, later, mirrored, *gathered, moved, *factors)
+    )(start, later, mirrored, *factors)
+
+
+def out_gradient_body(picks, *refs):
+    flows, factors = refs[: len(picks)], refs[len(picks) : 2 * len(picks)]
+    out_hbm, g_all, a_all, result, sem, out_sem = refs[2 * len(picks) :]
+    copy = pltpu.make_async_copy
+    copies = []
+    for index, pick in enumerate(picks):
+        copies.append(copy(factors[index].at[3], a_all.at[index], sem.at[0, index]))
+        copies.append(copy(flows[index].at[:, pick], g_all.at[index], sem.at[1, index]))
+    for one in copies:
+        one.start()
+    for one in copies:
+        one.wait()
+    rows, local = a_all.shape[1:]
+    features = g_all.shape[-1]
+    turned = a_all[...].reshape(len(picks) * rows, local).T
+    tile = features // 2
+    sent = []
+    for index in range(2):
+        cols = slice(index * tile, (index + 1) * tile)
+        upstream = g_all[:, :, :, cols].reshape(len(picks) * rows, tile)
+        result[:, cols] = dot_nn(turned, upstream).astype(jnp.bfloat16)
+        sent.append(copy(result.at[:, cols], out_hbm.at[:, cols], out_sem.at[index]))
+        sent[-1].start()
+    for one in sent:
+        one.wait()
+
+
+def out_gradient(flows, picks, factors):
+    shards, _, shard_rows, features = flows[0].shape
+    rows, local = factors[0].shape[1:]
+    count = len(picks)
+    return local_call(
+        functools.partial(out_gradient_body, picks),
+        jax.ShapeDtypeStruct((local, features), jnp.bfloat16),
+        (*flows, *factors),
+        flops=2 * count * rows * features * local,
+        moved=5 * MIB,
+        in_specs=[ANY] * (2 * count),
+        out_specs=ANY,
+        scratch=[
+            pltpu.VMEM((count, shards, shard_rows, features), jnp.bfloat16),
+            pltpu.VMEM((count, rows, local), jnp.bfloat16),
+            pltpu.VMEM((local, features), jnp.bfloat16),
+            pltpu.SemaphoreType.DMA((2, count)),
+            pltpu.SemaphoreType.DMA((2,)),
+        ],
+    )
 
 
 def after(value, *others):
@@ -455,6 +496,10 @@
             parts, row_up = lax.optimization_barrier((parts, row_up))
             mirrored = gathered_rows(jnp.concatenate([sent, row_up[None]], axis=0))
         parts = exchanged(parts)
+        if final:
+            mirrored_factors.append(lax.ppermute(factor_up, "section", across))
+            grad_qkv = qkv_gradient(start, later, mirrored, factors + mirrored_factors)
+            parts, grad_qkv = lax.optimization_barrier((parts, grad_qkv))
         y_up, y_down = layer_back(
             parts,
             (x_up, flow_up, ascending_loss_gradient),
@@ -480,9 +525,12 @@
                 row_up = lax.ppermute(row_up, "section", across)
                 gathered, factor_up, row_up = lax.optimization_barrier((gathered, factor_up, row_up))
                 added = [row_up]
-        mirrored_factors.append(lax.ppermute(factor_up, "section", across))
-    factors += mirrored_factors
-    grad_qkv, grad_out = gradients(start, later, mirrored, flows, parts, factors)
+            mirrored_factors.append(lax.ppermute(factor_up, "section", across))
+    grad_out = out_gradient(
+        (start, *flows, mirrored, mirrored, parts),
+        (3, 1, 1, TICKS, TICKS + 1, 2),
+        factors + mirrored_factors,
+    )
     return (
         jnp.transpose(grad_qkv, (1, 0, 2))[None],
         grad_out[None],

time: 272 us -> 265 us (0.974)
  starting transfers between devices: 56 us -> 50.9 us
  waiting for transfers between devices: 46.5 us -> 51.1 us
  Pallas kernels: 65.3 us -> 62.1 us
    ppermute x3, waiting for transfers between devices: 8.18 us -> 19.7 us  [per_device(): mirrored_factors.append(lax.ppermute(factor_up, 'section', across))]
    all_to_all x3, waiting for transfers between devices: 28.4 us -> 20.9 us  [exchanged(): return lax.all_to_all(parts, 'tp', split_axis=0, concat_axis=0, tiled=True)]
    ppermute x3, starting transfers between devices: 21.3 us -> 14.6 us  [per_device(): mirrored_factors.append(lax.ppermute(factor_up, 'section', across))]
    pallas_call x11 -> x12, Pallas kernels: 55.5 us -> 53.4 us  [local_call(): pl.pallas_call(body, out_shape=out_shape, in_specs=in_specs or [VMEM] * l...]
  transfers between devices with their start and end apart: 15 -> 15, of which waited for: 11 -> 13; matrix products, arithmetic and copies ran while one was open for 0% -> 0% of each run, Pallas kernels for 19% -> 20%
where the time goes in v2:
time: 265 us; the launch traced here: 264 us
  blocking collectives  82.9 us (31%)
  Pallas kernels  62.1 us (23%)
  waiting for transfers between devices  51.1 us (19%)
  starting transfers between devices  50.9 us (19%)
  between operations  14.2 us (5%)
    all_to_all x3, blocking collectives, exchanged(): return lax.all_to_all(parts, 'tp', split_axis=0, concat_axis=0, tiled=True)  82.9 us
    pallas_call x12, Pallas kernels, local_call(): pl.pallas_call(body, out_shape=out_shape, in_specs=in_specs or [VMEM] * l...  53.4 us
    all_to_all x3, waiting for transfers between devices, exchanged(): return lax.all_to_all(parts, 'tp', split_axis=0, concat_axis=0, tiled=True)  20.9 us
    ppermute x3, waiting for transfers between devices, per_device(): mirrored_factors.append(lax.ppermute(factor_up, 'section', across))  19.7 us
    ppermute x3, starting transfers between devices, per_device(): mirrored_factors.append(lax.ppermute(factor_up, 'section', across))  14.6 us
    all_to_all x3, starting transfers between devices, exchanged(): return lax.all_to_all(parts, 'tp', split_axis=0, concat_axis=0, tiled=True)  12.5 us
    ppermute x1, starting transfers between devices, per_device(): sent = lax.ppermute(sent, 'section', across)  10.1 us
    pallas_call x1, Pallas kernels, qkv_gradient(): pl.pallas_call(qkv_gradient_body, grid=(features // tile,), out_shape=jax...  8.65 us
  transfers between devices with their start and end apart: 15, of which 13 were waited for; matrix products, arithmetic and copies ran while one was open for 0% of the time, Pallas kernels for 20%

profile of v2, /device:TPU:1, one launch (start us, length us, event | category | flops | bytes accessed | tf_op | source)
XLA Modules:
  0.0 264.3 jit_solution(4710815326885928952)
XLA Ops:
  7.2 3.5 %shard_map.129 = (bf16[8,4,16,2048]{3,2,1,0:T(8,128)(2,1)}, bf16[4,16,2048]{2,1,0:T(8,128)(2,1)}, bf16[4,16,2048]{2,1,0:T(8,128)(2,1)}) custom-call(bf16[3,16,2048]{2,1,0:T(8,128)(2,1)} %bitcast.40, bf16[3,16,2048]{2,1,0:T(8,128)(2,1)} %bitcast.44, bf16[16,2048]{1,0:T(8,128)(2,1)} %bitcast.51, bf16[16,2048]{1,0:T(8,128)(2,1)} %bitcast.53), custom_call_target="tpu_custom_call" | custom-call | flops 3932 | bytes 983 | tf_op jit(solution)/shard_map/pallas_call | solution.py:39
  10.7 31.8 %all_to_all.30.h_hbm.g_hbm.start.refs_0_ = bf16[8,4,16,2048]{3,2,1,0:T(8,128)(2,1)} all-to-all(bf16[8,4,16,2048]{3,2,1,0:T(8,128)(2,1)} %get-tuple-element.55), channel_id=1, replica_groups=mesh['section'=32,'tp'=8] {'tp'}, dimensions={0} | all-to-all | bytes 4194304 | tf_op jit(solution)/shard_map/all_to_all | solution.py:442
  42.5 10.1 %collective-permute-start = (bf16[4,16,2048]{2,1,0:T(8,128)(2,1)S(1)}, bf16[4,16,2048]{2,1,0:T(8,128)(2,1)S(1)}, u32[]{:S(2)}, u32[]{:S(2)}) collective-permute-start(bf16[4,16,2048]{2,1,0:T(8,128)(2,1)S(1)} %copy-done.14), channel_id=1, source_target_pairs={{0,248},{8,240},{16,232},{24,224},{32,216},{40,208},{48,200},{56,1... | collective-permute-start | bytes 786440 | tf_op jit(solution)/shard_map/ppermute | solution.py:480
  52.6 5.2 %shard_map.130 = (bf16[2,4,128,256]{3,2,1,0:T(8,128)(2,1)}, f32[2,2,128,128]{3,2,1,0:T(8,128)}) custom-call(bf16[8,4,16,2048]{3,2,1,0:T(8,128)(2,1)} %all_to_all.30.h_hbm.g_hbm.start.refs_0_, bf16[3,2048,256]{2,1,0:T(8,128)(2,1)} %bitcast.21, bf16[3,2048,256]{2,1,0:T(8,128)(2,1)} %bitcast.26), custom_call_target="tpu_custom_call" | custom-call | flops 805306 | bytes 8388 | tf_op jit(solution)/shard_map/pallas_call | solution.py:39
  57.8 6.9 %shard_map.131 = (bf16[8,2,16,2048]{3,2,1,0:T(8,128)(2,1)}, bf16[4,128,256]{2,1,0:T(8,128)(2,1)}, bf16[4,128,256]{2,1,0:T(8,128)(2,1)}) custom-call(bf16[8,4,16,2048]{3,2,1,0:T(8,128)(2,1)} %all_to_all.30.h_hbm.g_hbm.start.refs_0_, bf16[2,4,128,256]{3,2,1,0:T(8,128)(2,1)} %get-tuple-element.59.qkv_hbm, f32[2,2,128,128]{3,2,1,0:T(8,128)} %get-tuple-element.60.soft_hbm, ...), custom_call_target="tpu_custom_call" | custom-call | flops 1073741 | bytes 12582 | tf_op jit(solution)/shard_map/pallas_call | solution.py:39
  64.9 26.4 %all_to_all.31.parts_ref = bf16[8,2,16,2048]{3,2,1,0:T(8,128)(2,1)} all-to-all(bf16[8,2,16,2048]{3,2,1,0:T(8,128)(2,1)} %get-tuple-element.63), channel_id=1, replica_groups=mesh['section'=32,'tp'=8] {'tp'}, dimensions={0} | all-to-all | bytes 2097152 | tf_op jit(solution)/shard_map/all_to_all | solution.py:442
  91.3 2.6 shard_map.132
  97.2 2.5 collective-permute-done.2.refs_1_.refs_4_
  100.4 2.0 shard_map.133
  102.4 3.9 %all-to-all-start.2 = ((bf16[8,2,16,2048]{3,2,1,0:T(8,128)(2,1)}), bf16[8,2,16,2048]{3,2,1,0:T(8,128)(2,1)S(1)}, u32[]{:S(2)}, u32[]{:S(2)}) async-start(bf16[8,2,16,2048]{3,2,1,0:T(8,128)(2,1)} %shard_map.133), calls=%async_computation.2 | async-start | bytes 2097152 | tf_op jit(solution)/shard_map/all_to_all | solution.py:442
  106.4 7.4 %shard_map.134 = (bf16[2,4,128,256]{3,2,1,0:T(8,128)(2,1)}, f32[2,2,128,128]{3,2,1,0:T(8,128)}, bf16[2,4,128,256]{3,2,1,0:T(8,128)(2,1)}, f32[2,2,128,128]{3,2,1,0:T(8,128)}) custom-call(bf16[8,4,16,2048]{3,2,1,0:T(8,128)(2,1)} %bitcast.48, bf16[3,2048,256]{2,1,0:T(8,128)(2,1)} %bitcast.23, bf16[3,2048,256]{2,1,0:T(8,128)(2,1)} %bitcast.28), custom_call_target="tpu_custom_call" | custom-call | flops 1610612 | bytes 8388 | tf_op jit(solution)/shard_map/pallas_call | solution.py:39
  113.7 6.9 %all-to-all-done.2.g_hbm.refs_1_ = bf16[8,2,16,2048]{3,2,1,0:T(8,128)(2,1)S(1)} async-done(((bf16[8,2,16,2048]{3,2,1,0:T(8,128)(2,1)}), bf16[8,2,16,2048]{3,2,1,0:T(8,128)(2,1)S(1)}, u32[]{:S(2)}, u32[]{:S(2)}) %all-to-all-start.2) | async-done | bytes 1048608 | tf_op jit(solution)/shard_map/all_to_all | solution.py:442
  120.6 9.1 %collective-permute-start.3 = (bf16[4,128,256]{2,1,0:T(8,128)(2,1)S(1)}, bf16[4,128,256]{2,1,0:T(8,128)(2,1)S(1)}, u32[]{:S(2)}, u32[]{:S(2)}) collective-permute-start(bf16[4,128,256]{2,1,0:T(8,128)(2,1)S(1)} %copy-done.13), channel_id=1, source_target_pairs={{0,248},{8,240},{16,232},{24,224},{32,216},{40,208},{48,200},{56,1... | collective-permute-start | bytes 786440 | tf_op jit(solution)/shard_map/ppermute | solution.py:528
  130.1 6.9 %shard_map.135 = (bf16[8,2,16,2048]{3,2,1,0:T(8,128)(2,1)}, bf16[4,128,256]{2,1,0:T(8,128)(2,1)}, bf16[4,128,256]{2,1,0:T(8,128)(2,1)}) custom-call(bf16[8,2,16,2048]{3,2,1,0:T(8,128)(2,1)} %copy-done, bf16[2,4,128,256]{3,2,1,0:T(8,128)(2,1)} %get-tuple-element.75.qkv_hbm, f32[2,2,128,128]{3,2,1,0:T(8,128)} %get-tuple-element.76.soft_hbm, ...), custom_call_target="tpu_custom_call" | custom-call | flops 1073741 | bytes 12582 | tf_op jit(solution)/shard_map/pallas_call | solution.py:39
  137.0 5.9 %collective-permute-done.3.rest_3_.refs_9_ = bf16[4,128,256]{2,1,0:T(8,128)(2,1)S(1)} collective-permute-done((bf16[4,128,256]{2,1,0:T(8,128)(2,1)S(1)}, bf16[4,128,256]{2,1,0:T(8,128)(2,1)S(1)}, u32[]{:S(2)}, u32[]{:S(2)}) %collective-permute-start.3) | collective-permute-done | bytes 262176 | tf_op jit(solution)/shard_map/ppermute | solution.py:528
  145.0 24.6 %all_to_all.32.parts_ref = bf16[8,2,16,2048]{3,2,1,0:T(8,128)(2,1)} all-to-all(bf16[8,2,16,2048]{3,2,1,0:T(8,128)(2,1)} %get-tuple-element.81), channel_id=1, replica_groups=mesh['section'=32,'tp'=8] {'tp'}, dimensions={0} | all-to-all | bytes 2097152 | tf_op jit(solution)/shard_map/all_to_all | solution.py:442
  169.6 2.6 shard_map.136
  172.2 3.9 %collective-permute-start.6 = (bf16[16,2048]{1,0:T(8,128)(2,1)}, bf16[16,2048]{1,0:T(8,128)(2,1)S(1)}, u32[]{:S(2)}, u32[]{:S(2)}) collective-permute-start(bf16[16,2048]{1,0:T(8,128)(2,1)} %get-tuple-element.83), channel_id=1, source_target_pairs={{0,248},{8,0},{16,8},{24,16},{32,24},{40,32},{48,40},{56,48},{64,5... | collective-permute-start | bytes 196616 | tf_op jit(solution)/shard_map/ppermute | solution.py:512
  178.3 2.0 shard_map.137
  180.3 4.4 %all-to-all-start.4 = ((bf16[8,2,16,2048]{3,2,1,0:T(8,128)(2,1)}), bf16[8,2,16,2048]{3,2,1,0:T(8,128)(2,1)S(1)}, u32[]{:S(2)}, u32[]{:S(2)}) async-start(bf16[8,2,16,2048]{3,2,1,0:T(8,128)(2,1)} %shard_map.137), calls=%async_computation.4 | async-start | bytes 2097152 | tf_op jit(solution)/shard_map/all_to_all | solution.py:442
  184.6 7.6 %collective-permute-start.7 = (bf16[16,2048]{1,0:T(8,128)(2,1)S(1)}, bf16[16,2048]{1,0:T(8,128)(2,1)S(1)}, u32[]{:S(2)}, u32[]{:S(2)}) collective-permute-start(bf16[16,2048]{1,0:T(8,128)(2,1)S(1)} %copy-done.3), channel_id=1, source_target_pairs={{0,248},{8,240},{16,232},{24,224},{32,216},{40,208},{48,200},{56,1... | collective-permute-start | bytes 196616 | tf_op jit(solution)/shard_map/ppermute | solution.py:525
  192.3 3.7 %collective-permute-done.7.rest_0_ = bf16[16,2048]{1,0:T(8,128)(2,1)S(1)} collective-permute-done((bf16[16,2048]{1,0:T(8,128)(2,1)S(1)}, bf16[16,2048]{1,0:T(8,128)(2,1)S(1)}, u32[]{:S(2)}, u32[]{:S(2)}) %collective-permute-start.7) | collective-permute-done | bytes 65568 | tf_op jit(solution)/shard_map/ppermute | solution.py:525
  195.9 8.2 %all-to-all-done.4.g_hbm.refs_2_ = bf16[8,2,16,2048]{3,2,1,0:T(8,128)(2,1)S(1)} async-done(((bf16[8,2,16,2048]{3,2,1,0:T(8,128)(2,1)}), bf16[8,2,16,2048]{3,2,1,0:T(8,128)(2,1)S(1)}, u32[]{:S(2)}, u32[]{:S(2)}) %all-to-all-start.4) | async-done | bytes 1048608 | tf_op jit(solution)/shard_map/all_to_all | solution.py:442
  204.1 4.1 %collective-permute-start.8 = (bf16[4,128,256]{2,1,0:T(8,128)(2,1)S(1)}, bf16[4,128,256]{2,1,0:T(8,128)(2,1)S(1)}, u32[]{:S(2)}, u32[]{:S(2)}) collective-permute-start(bf16[4,128,256]{2,1,0:T(8,128)(2,1)S(1)} %copy-done.12), channel_id=1, source_target_pairs={{0,248},{8,240},{16,232},{24,224},{32,216},{40,208},{48,200},{56,1... | collective-permute-start | bytes 786440 | tf_op jit(solution)/shard_map/ppermute | solution.py:528
  208.2 8.0 %shard_map.138 = (bf16[8,3,16,2048]{3,2,1,0:T(8,128)(2,1)}, bf16[4,128,256]{2,1,0:T(8,128)(2,1)}, bf16[4,128,256]{2,1,0:T(8,128)(2,1)}) custom-call(bf16[8,2,16,2048]{3,2,1,0:T(8,128)(2,1)} %copy-done.1, bf16[2,4,128,256]{3,2,1,0:T(8,128)(2,1)} %get-tuple-element.88.qkv_hbm, f32[2,2,128,128]{3,2,1,0:T(8,128)} %get-tuple-element.89.soft_hbm, ...), custom_call_target="tpu_custom_call" | custom-call | flops 1073741 | bytes 12582 | tf_op jit(solution)/shard_map/pallas_call | solution.py:39
  217.6 7.5 %collective-permute-done.8.rest_4_.refs_10_ = bf16[4,128,256]{2,1,0:T(8,128)(2,1)S(1)} collective-permute-done((bf16[4,128,256]{2,1,0:T(8,128)(2,1)S(1)}, bf16[4,128,256]{2,1,0:T(8,128)(2,1)S(1)}, u32[]{:S(2)}, u32[]{:S(2)}) %collective-permute-start.8) | collective-permute-done | bytes 262176 | tf_op jit(solution)/shard_map/ppermute | solution.py:528
  225.0 4.3 %all-to-all-start.5 = ((bf16[8,3,16,2048]{3,2,1,0:T(8,128)(2,1)}), bf16[8,3,16,2048]{3,2,1,0:T(8,128)(2,1)}, u32[]{:S(2)}, u32[]{:S(2)}) async-start(bf16[8,3,16,2048]{3,2,1,0:T(8,128)(2,1)} %get-tuple-element.93), calls=%async_computation.5 | async-start | bytes 3145728 | tf_op jit(solution)/shard_map/all_to_all | solution.py:442
  229.3 6.4 %collective-permute-done.9.rest_5_.refs_11_ = bf16[4,128,256]{2,1,0:T(8,128)(2,1)S(1)} collective-permute-done((bf16[4,128,256]{2,1,0:T(8,128)(2,1)}, bf16[4,128,256]{2,1,0:T(8,128)(2,1)S(1)}, u32[]{:S(2)}, u32[]{:S(2)}) %collective-permute-start.9) | collective-permute-done | bytes 262176 | tf_op jit(solution)/shard_map/ppermute | solution.py:500
  236.4 8.6 %shard_map.139 = bf16[3,2048,256]{2,1,0:T(8,128)(2,1)} custom-call(bf16[8,4,16,2048]{3,2,1,0:T(8,128)(2,1)} %all_to_all.30.h_hbm.g_hbm.start.refs_0_, bf16[8,4,16,2048]{3,2,1,0:T(8,128)(2,1)} %bitcast.49, bf16[8,5,16,2048]{3,2,1,0:T(8,128)(2,1)} %bitcast.31, bf16[4,128,256]{2,1,0:T(8,128)(2,1)} %get-tuple-element.96.rest_0_.refs_6_, ...), custom_call_target="tpu_custom_call" | custom-call | flops 241591910400 | bytes 838860800 | tf_op jit(solution)/shard_map/pallas_call | solution.py:374
  245.0 5.8 %all-to-all-done.5.refs_5_.parts_ref = bf16[8,3,16,2048]{3,2,1,0:T(8,128)(2,1)} async-done(((bf16[8,3,16,2048]{3,2,1,0:T(8,128)(2,1)}), bf16[8,3,16,2048]{3,2,1,0:T(8,128)(2,1)}, u32[]{:S(2)}, u32[]{:S(2)}) %all-to-all-start.5) | async-done | bytes 1572896 | tf_op jit(solution)/shard_map/all_to_all | solution.py:442
  250.8 3.9 %shard_map.140 = bf16[256,2048]{1,0:T(8,128)(2,1)} custom-call(bf16[8,4,16,2048]{3,2,1,0:T(8,128)(2,1)} %all_to_all.30.h_hbm.g_hbm.start.refs_0_, bf16[8,2,16,2048]{3,2,1,0:T(8,128)(2,1)} %copy-done, bf16[8,2,16,2048]{3,2,1,0:T(8,128)(2,1)} %copy-done.1, bf16[8,5,16,2048]{3,2,1,0:T(8,128)(2,1)} %bitcast.32, bf16[8,5,16,2048]{3,2,1,0:T(8,128)(2,1)} %bitcast.33, ...), custom_call_target="tpu_custom_call" | custom-call | flops 805306 | bytes 5242 | tf_op jit(solution)/shard_map/pallas_call | solution.py:39
  254.7 2.7 %shard_map.141 = (bf16[16,2048]{1,0:T(8,128)(2,1)}, bf16[16,2048]{1,0:T(8,128)(2,1)}) custom-call(bf16[8,3,16,2048]{3,2,1,0:T(8,128)(2,1)} %all-to-all-done.5.refs_5_.parts_ref, bf16[3,16,2048]{2,1,0:T(8,128)(2,1)} %bitcast.47, bf16[16,2048]{1,0:T(8,128)(2,1)} %copy-done.2, bf16[2,16,2048]{2,1,0:T(8,128)(2,1)} %refs_2_.5, bf16[3,16,2048]{2,1,0:T(8,128)(2,1)} %bitcast.43, ...), custom_call_target="tpu_custom_call" | custom-call | flops 15728 | bytes 2359 | tf_op jit(solution)/shard_map/pallas_call | solution.py:39
  (47 shorter events, 10.9 us)
Async XLA Ops:
  7.2 99.2 %all-gather.5.cloned.1.call-start = ((), (), s32[]{:S(2)}) async-start(), calls=%async_computation.6 | async-start | bytes 2359296 | tf_op jit(solution)/shard_map/all_gather | solution.py:446
  10.7 31.8 %copy-start.14 = (bf16[4,16,2048]{2,1,0:T(8,128)(2,1)S(1)}, bf16[4,16,2048]{2,1,0:T(8,128)(2,1)}, u32[]{:S(2)}) copy-start(bf16[4,16,2048]{2,1,0:T(8,128)(2,1)} %get-tuple-element.62) | copy-start | bytes 786436
  42.5 22.3 %collective-permute-start = (bf16[4,16,2048]{2,1,0:T(8,128)(2,1)S(1)}, bf16[4,16,2048]{2,1,0:T(8,128)(2,1)S(1)}, u32[]{:S(2)}, u32[]{:S(2)}) collective-permute-start(bf16[4,16,2048]{2,1,0:T(8,128)(2,1)S(1)} %copy-done.14), channel_id=1, source_target_pairs={{0,248},{8,240},{16,232},{24,224},{32,216},{40,208},{48,200},{56,1... | collective-permute-start | bytes 786440 | tf_op jit(solution)/shard_map/ppermute | solution.py:480
  93.9 3.3 %collective-permute-start.1 = (bf16[16,2048]{1,0:T(8,128)(2,1)}, bf16[16,2048]{1,0:T(8,128)(2,1)S(1)}, u32[]{:S(2)}, u32[]{:S(2)}) collective-permute-start(bf16[16,2048]{1,0:T(8,128)(2,1)} %get-tuple-element.64), channel_id=1, source_target_pairs={{0,8},{8,16},{16,24},{24,32},{32,40},{40,48},{48,56},{56,64},{64,7... | collective-permute-start | bytes 196616 | tf_op jit(solution)/shard_map/ppermute | solution.py:511
  95.6 4.2 %collective-permute-start.2 = (bf16[16,2048]{1,0:T(8,128)(2,1)}, bf16[16,2048]{1,0:T(8,128)(2,1)S(1)}, u32[]{:S(2)}, u32[]{:S(2)}) collective-permute-start(bf16[16,2048]{1,0:T(8,128)(2,1)} %get-tuple-element.65), channel_id=1, source_target_pairs={{0,248},{8,0},{16,8},{24,16},{32,24},{40,32},{48,40},{56,48},{64,5... | collective-permute-start | bytes 196616 | tf_op jit(solution)/shard_map/ppermute | solution.py:512
  97.2 2.6 copy-start.5
  99.8 0.6 copy-start.7
  102.4 18.2 %all-to-all-start.2 = ((bf16[8,2,16,2048]{3,2,1,0:T(8,128)(2,1)}), bf16[8,2,16,2048]{3,2,1,0:T(8,128)(2,1)S(1)}, u32[]{:S(2)}, u32[]{:S(2)}) async-start(bf16[8,2,16,2048]{3,2,1,0:T(8,128)(2,1)} %shard_map.133), calls=%async_computation.2 | async-start | bytes 2097152 | tf_op jit(solution)/shard_map/all_to_all | solution.py:442
  106.3 129.4 %all-gather.7.cloned.1.call-start = ((), (), s32[]{:S(2)}) async-start(), calls=%async_computation.7 | async-start | bytes 2949120 | tf_op jit(solution)/shard_map/all_gather | solution.py:446
  106.3 14.3 %copy-start.13 = (bf16[4,128,256]{2,1,0:T(8,128)(2,1)S(1)}, bf16[4,128,256]{2,1,0:T(8,128)(2,1)}, u32[]{:S(2)}) copy-start(bf16[4,128,256]{2,1,0:T(8,128)(2,1)} %get-tuple-element.78) | copy-start | bytes 786436
  106.4 23.4 %copy-start.6 = (bf16[16,2048]{1,0:T(8,128)(2,1)S(1)}, bf16[16,2048]{1,0:T(8,128)(2,1)}, u32[]{:S(2)}) copy-start(bf16[16,2048]{1,0:T(8,128)(2,1)} %copy-done.5) | copy-start | bytes 196612
  120.6 9.4 %copy-start = (bf16[8,2,16,2048]{3,2,1,0:T(8,128)(2,1)}, bf16[8,2,16,2048]{3,2,1,0:T(8,128)(2,1)S(1)}, u32[]{:S(2)}) copy-start(bf16[8,2,16,2048]{3,2,1,0:T(8,128)(2,1)S(1)} %all-to-all-done.2.g_hbm.refs_1_) | copy-start | bytes 3145732
  120.6 22.2 %collective-permute-start.3 = (bf16[4,128,256]{2,1,0:T(8,128)(2,1)S(1)}, bf16[4,128,256]{2,1,0:T(8,128)(2,1)S(1)}, u32[]{:S(2)}, u32[]{:S(2)}) collective-permute-start(bf16[4,128,256]{2,1,0:T(8,128)(2,1)S(1)} %copy-done.13), channel_id=1, source_target_pairs={{0,248},{8,240},{16,232},{24,224},{32,216},{40,208},{48,200},{56,1... | collective-permute-start | bytes 786440 | tf_op jit(solution)/shard_map/ppermute | solution.py:528
  129.8 14.4 %collective-permute-start.4 = (bf16[16,2048]{1,0:T(8,128)(2,1)S(1)}, bf16[16,2048]{1,0:T(8,128)(2,1)S(1)}, u32[]{:S(2)}, u32[]{:S(2)}) collective-permute-start(bf16[16,2048]{1,0:T(8,128)(2,1)S(1)} %copy-done.6), channel_id=1, source_target_pairs={{0,248},{8,240},{16,232},{24,224},{32,216},{40,208},{48,200},{56,1... | collective-permute-start | bytes 196616 | tf_op jit(solution)/shard_map/ppermute | solution.py:523
  142.9 29.3 %copy-start.8 = (bf16[4,128,256]{2,1,0:T(8,128)(2,1)}, bf16[4,128,256]{2,1,0:T(8,128)(2,1)S(1)}, u32[]{:S(2)}) copy-start(bf16[4,128,256]{2,1,0:T(8,128)(2,1)S(1)} %collective-permute-done.3.rest_3_.refs_9_) | copy-start | bytes 786436
  172.2 31.9 %copy-start.12 = (bf16[4,128,256]{2,1,0:T(8,128)(2,1)S(1)}, bf16[4,128,256]{2,1,0:T(8,128)(2,1)}, u32[]{:S(2)}) copy-start(bf16[4,128,256]{2,1,0:T(8,128)(2,1)} %get-tuple-element.92) | copy-start | bytes 786436
  172.2 4.9 %collective-permute-start.5 = (bf16[16,2048]{1,0:T(8,128)(2,1)}, bf16[16,2048]{1,0:T(8,128)(2,1)S(1)}, u32[]{:S(2)}, u32[]{:S(2)}) collective-permute-start(bf16[16,2048]{1,0:T(8,128)(2,1)} %get-tuple-element.82), channel_id=1, source_target_pairs={{0,8},{8,16},{16,24},{24,32},{32,40},{40,48},{48,56},{56,64},{64,7... | collective-permute-start | bytes 196616 | tf_op jit(solution)/shard_map/ppermute | solution.py:511
  172.2 5.1 %collective-permute-start.6 = (bf16[16,2048]{1,0:T(8,128)(2,1)}, bf16[16,2048]{1,0:T(8,128)(2,1)S(1)}, u32[]{:S(2)}, u32[]{:S(2)}) collective-permute-start(bf16[16,2048]{1,0:T(8,128)(2,1)} %get-tuple-element.83), channel_id=1, source_target_pairs={{0,248},{8,0},{16,8},{24,16},{32,24},{40,32},{48,40},{56,48},{64,5... | collective-permute-start | bytes 196616 | tf_op jit(solution)/shard_map/ppermute | solution.py:512
  177.1 0.6 copy-start.2
  177.7 0.6 copy-start.4
  180.3 4.4 %copy-start.3 = (bf16[16,2048]{1,0:T(8,128)(2,1)S(1)}, bf16[16,2048]{1,0:T(8,128)(2,1)}, u32[]{:S(2)}) copy-start(bf16[16,2048]{1,0:T(8,128)(2,1)} %copy-done.2) | copy-start | bytes 196612
  180.3 23.8 %all-to-all-start.4 = ((bf16[8,2,16,2048]{3,2,1,0:T(8,128)(2,1)}), bf16[8,2,16,2048]{3,2,1,0:T(8,128)(2,1)S(1)}, u32[]{:S(2)}, u32[]{:S(2)}) async-start(bf16[8,2,16,2048]{3,2,1,0:T(8,128)(2,1)} %shard_map.137), calls=%async_computation.4 | async-start | bytes 2097152 | tf_op jit(solution)/shard_map/all_to_all | solution.py:442
  184.6 11.3 %collective-permute-start.7 = (bf16[16,2048]{1,0:T(8,128)(2,1)S(1)}, bf16[16,2048]{1,0:T(8,128)(2,1)S(1)}, u32[]{:S(2)}, u32[]{:S(2)}) collective-permute-start(bf16[16,2048]{1,0:T(8,128)(2,1)S(1)} %copy-done.3), channel_id=1, source_target_pairs={{0,248},{8,240},{16,232},{24,224},{32,216},{40,208},{48,200},{56,1... | collective-permute-start | bytes 196616 | tf_op jit(solution)/shard_map/ppermute | solution.py:525
  195.9 12.3 %copy-start.11 = (bf16[16,2048]{1,0:T(8,128)(2,1)}, bf16[16,2048]{1,0:T(8,128)(2,1)S(1)}, u32[]{:S(2)}) copy-start(bf16[16,2048]{1,0:T(8,128)(2,1)S(1)} %collective-permute-done.7.rest_0_) | copy-start | bytes 196612
  204.1 4.1 %copy-start.1 = (bf16[8,2,16,2048]{3,2,1,0:T(8,128)(2,1)}, bf16[8,2,16,2048]{3,2,1,0:T(8,128)(2,1)S(1)}, u32[]{:S(2)}) copy-start(bf16[8,2,16,2048]{3,2,1,0:T(8,128)(2,1)S(1)} %all-to-all-done.4.g_hbm.refs_2_) | copy-start | bytes 3145732
  204.1 20.9 %collective-permute-start.8 = (bf16[4,128,256]{2,1,0:T(8,128)(2,1)S(1)}, bf16[4,128,256]{2,1,0:T(8,128)(2,1)S(1)}, u32[]{:S(2)}, u32[]{:S(2)}) collective-permute-start(bf16[4,128,256]{2,1,0:T(8,128)(2,1)S(1)} %copy-done.12), channel_id=1, source_target_pairs={{0,248},{8,240},{16,232},{24,224},{32,216},{40,208},{48,200},{56,1... | collective-permute-start | bytes 786440 | tf_op jit(solution)/shard_map/ppermute | solution.py:528
  216.2 19.5 %collective-permute-start.9 = (bf16[4,128,256]{2,1,0:T(8,128)(2,1)}, bf16[4,128,256]{2,1,0:T(8,128)(2,1)S(1)}, u32[]{:S(2)}, u32[]{:S(2)}) collective-permute-start(bf16[4,128,256]{2,1,0:T(8,128)(2,1)} %get-tuple-element.101), channel_id=1, source_target_pairs={{0,248},{8,240},{16,232},{24,224},{32,216},{40,208},{48,200},{56,1... | collective-permute-start | bytes 786440 | tf_op jit(solution)/shard_map/ppermute | solution.py:500
  225.0 10.7 %copy-start.9 = (bf16[4,128,256]{2,1,0:T(8,128)(2,1)}, bf16[4,128,256]{2,1,0:T(8,128)(2,1)S(1)}, u32[]{:S(2)}) copy-start(bf16[4,128,256]{2,1,0:T(8,128)(2,1)S(1)} %collective-permute-done.8.rest_4_.refs_10_) | copy-start | bytes 786436
  225.0 25.8 %all-to-all-start.5 = ((bf16[8,3,16,2048]{3,2,1,0:T(8,128)(2,1)}), bf16[8,3,16,2048]{3,2,1,0:T(8,128)(2,1)}, u32[]{:S(2)}, u32[]{:S(2)}) async-start(bf16[8,3,16,2048]{3,2,1,0:T(8,128)(2,1)} %get-tuple-element.93), calls=%async_computation.5 | async-start | bytes 3145728 | tf_op jit(solution)/shard_map/all_to_all | solution.py:442
  235.7 0.7 copy-start.10
Sparse Core Ops, SparseCore 0:
  42.6 52.1 all-gather.4
  145.1 46.8 all-gather.6

commit v3 on v2

--- a/solution.py
+++ b/solution.py
@@ -515,14 +515,13 @@
             gathered = exchanged(gathered)
             picks = (0, 1)
             flows.append(gathered)
+            row_up = lax.ppermute(row_up, "section", across)
             if tick == 0:
                 saved += forward(later, ((2, 3), (0, 1)), w_up, w_down)
                 gathered, row_up, factor_up, saved[1:] = lax.optimization_barrier(
                     (gathered, row_up, factor_up, saved[1:])
                 )
-                row_up = lax.ppermute(row_up, "section", across)
             else:
-                row_up = lax.ppermute(row_up, "section", across)
                 gathered, factor_up, row_up = lax.optimization_barrier((gathered, factor_up, row_up))
                 added = [row_up]
             mirrored_factors.append(lax.ppermute(factor_up, "section", across))

time: 265 us -> 261 us (0.985)
  waiting for transfers between devices: 51.1 us -> 42.3 us
  starting transfers between devices: 50.9 us -> 56.3 us
    all_to_all x3, waiting for transfers between devices: 20.9 us -> 15.6 us  [exchanged(): return lax.all_to_all(parts, 'tp', split_axis=0, concat_axis=0, tiled=True)]
    ppermute x2, starting transfers between devices: 7.92 us -> 12.6 us  [per_device(): row_up = lax.ppermute(row_up, 'section', across)]
  transfers between devices with their start and end apart: 15 -> 15, of which waited for: 13 -> 12; matrix products, arithmetic and copies ran while one was open for 0% -> 0% of each run, Pallas kernels for 20% -> 20%
where the time goes in v3:
time: 261 us; the launch traced here: 260 us
  blocking collectives  82.2 us (31%)
  Pallas kernels  62.1 us (24%)
  starting transfers between devices  56.3 us (22%)
  waiting for transfers between devices  42.3 us (16%)
  between operations  14.2 us (5%)
    all_to_all x3, blocking collectives, exchanged(): return lax.all_to_all(parts, 'tp', split_axis=0, concat_axis=0, tiled=True)  82.2 us
    pallas_call x12, Pallas kernels, local_call(): pl.pallas_call(body, out_shape=out_shape, in_specs=in_specs or [VMEM] * l...  53.4 us
    ppermute x3, waiting for transfers between devices, per_device(): mirrored_factors.append(lax.ppermute(factor_up, 'section', across))  18 us
    all_to_all x3, waiting for transfers between devices, exchanged(): return lax.all_to_all(parts, 'tp', split_axis=0, concat_axis=0, tiled=True)  15.6 us
    ppermute x3, starting transfers between devices, per_device(): mirrored_factors.append(lax.ppermute(factor_up, 'section', across))  14.1 us
    ppermute x2, starting transfers between devices, per_device(): row_up = lax.ppermute(row_up, 'section', across)  12.6 us
    all_to_all x3, starting transfers between devices, exchanged(): return lax.all_to_all(parts, 'tp', split_axis=0, concat_axis=0, tiled=True)  12 us
    ppermute x1, starting transfers between devices, per_device(): sent = lax.ppermute(sent, 'section', across)  10.1 us
  transfers between devices with their start and end apart: 15, of which 12 were waited for; matrix products, arithmetic and copies ran while one was open for 0% of the time, Pallas kernels for 20%

profile of v3, /device:TPU:1, one launch (start us, length us, event | category | flops | bytes accessed | tf_op | source)
XLA Modules:
  0.0 260.3 jit_solution(4739178950438232051)
XLA Ops:
  7.2 3.5 %shard_map.129 = (bf16[8,4,16,2048]{3,2,1,0:T(8,128)(2,1)}, bf16[4,16,2048]{2,1,0:T(8,128)(2,1)}, bf16[4,16,2048]{2,1,0:T(8,128)(2,1)}) custom-call(bf16[3,16,2048]{2,1,0:T(8,128)(2,1)} %bitcast.40, bf16[3,16,2048]{2,1,0:T(8,128)(2,1)} %bitcast.44, bf16[16,2048]{1,0:T(8,128)(2,1)} %bitcast.51, bf16[16,2048]{1,0:T(8,128)(2,1)} %bitcast.53), custom_call_target="tpu_custom_call" | custom-call | flops 3932 | bytes 983 | tf_op jit(solution)/shard_map/pallas_call | solution.py:39
  10.7 31.8 %all_to_all.30.h_hbm.g_hbm.start.refs_0_ = bf16[8,4,16,2048]{3,2,1,0:T(8,128)(2,1)} all-to-all(bf16[8,4,16,2048]{3,2,1,0:T(8,128)(2,1)} %get-tuple-element.55), channel_id=1, replica_groups=mesh['section'=32,'tp'=8] {'tp'}, dimensions={0} | all-to-all | bytes 4194304 | tf_op jit(solution)/shard_map/all_to_all | solution.py:442
  42.5 10.1 %collective-permute-start = (bf16[4,16,2048]{2,1,0:T(8,128)(2,1)S(1)}, bf16[4,16,2048]{2,1,0:T(8,128)(2,1)S(1)}, u32[]{:S(2)}, u32[]{:S(2)}) collective-permute-start(bf16[4,16,2048]{2,1,0:T(8,128)(2,1)S(1)} %copy-done.14), channel_id=1, source_target_pairs={{0,248},{8,240},{16,232},{24,224},{32,216},{40,208},{48,200},{56,1... | collective-permute-start | bytes 786440 | tf_op jit(solution)/shard_map/ppermute | solution.py:480
  52.6 5.2 %shard_map.130 = (bf16[2,4,128,256]{3,2,1,0:T(8,128)(2,1)}, f32[2,2,128,128]{3,2,1,0:T(8,128)}) custom-call(bf16[8,4,16,2048]{3,2,1,0:T(8,128)(2,1)} %all_to_all.30.h_hbm.g_hbm.start.refs_0_, bf16[3,2048,256]{2,1,0:T(8,128)(2,1)} %bitcast.21, bf16[3,2048,256]{2,1,0:T(8,128)(2,1)} %bitcast.26), custom_call_target="tpu_custom_call" | custom-call | flops 805306 | bytes 8388 | tf_op jit(solution)/shard_map/pallas_call | solution.py:39
  57.8 6.9 %shard_map.131 = (bf16[8,2,16,2048]{3,2,1,0:T(8,128)(2,1)}, bf16[4,128,256]{2,1,0:T(8,128)(2,1)}, bf16[4,128,256]{2,1,0:T(8,128)(2,1)}) custom-call(bf16[8,4,16,2048]{3,2,1,0:T(8,128)(2,1)} %all_to_all.30.h_hbm.g_hbm.start.refs_0_, bf16[2,4,128,256]{3,2,1,0:T(8,128)(2,1)} %get-tuple-element.59.qkv_hbm, f32[2,2,128,128]{3,2,1,0:T(8,128)} %get-tuple-element.60.soft_hbm, ...), custom_call_target="tpu_custom_call" | custom-call | flops 1073741 | bytes 12582 | tf_op jit(solution)/shard_map/pallas_call | solution.py:39
  64.9 26.4 %all_to_all.31.parts_ref = bf16[8,2,16,2048]{3,2,1,0:T(8,128)(2,1)} all-to-all(bf16[8,2,16,2048]{3,2,1,0:T(8,128)(2,1)} %get-tuple-element.63), channel_id=1, replica_groups=mesh['section'=32,'tp'=8] {'tp'}, dimensions={0} | all-to-all | bytes 2097152 | tf_op jit(solution)/shard_map/all_to_all | solution.py:442
  91.3 2.6 shard_map.132
  97.2 2.5 collective-permute-done.2.refs_1_.refs_4_
  100.4 2.0 shard_map.133
  102.4 4.0 %all-to-all-start.2 = ((bf16[8,2,16,2048]{3,2,1,0:T(8,128)(2,1)}), bf16[8,2,16,2048]{3,2,1,0:T(8,128)(2,1)S(1)}, u32[]{:S(2)}, u32[]{:S(2)}) async-start(bf16[8,2,16,2048]{3,2,1,0:T(8,128)(2,1)} %shard_map.133), calls=%async_computation.2 | async-start | bytes 2097152 | tf_op jit(solution)/shard_map/all_to_all | solution.py:442
  106.5 6.9 %collective-permute-start.3 = (bf16[16,2048]{1,0:T(8,128)(2,1)S(1)}, bf16[16,2048]{1,0:T(8,128)(2,1)S(1)}, u32[]{:S(2)}, u32[]{:S(2)}) collective-permute-start(bf16[16,2048]{1,0:T(8,128)(2,1)S(1)} %copy-done.6), channel_id=1, source_target_pairs={{0,248},{8,240},{16,232},{24,224},{32,216},{40,208},{48,200},{56,1... | collective-permute-start | bytes 196616 | tf_op jit(solution)/shard_map/ppermute | solution.py:518
  113.4 7.4 %shard_map.134 = (bf16[2,4,128,256]{3,2,1,0:T(8,128)(2,1)}, f32[2,2,128,128]{3,2,1,0:T(8,128)}, bf16[2,4,128,256]{3,2,1,0:T(8,128)(2,1)}, f32[2,2,128,128]{3,2,1,0:T(8,128)}) custom-call(bf16[8,4,16,2048]{3,2,1,0:T(8,128)(2,1)} %bitcast.48, bf16[3,2048,256]{2,1,0:T(8,128)(2,1)} %bitcast.23, bf16[3,2048,256]{2,1,0:T(8,128)(2,1)} %bitcast.28), custom_call_target="tpu_custom_call" | custom-call | flops 1610612 | bytes 8388 | tf_op jit(solution)/shard_map/pallas_call | solution.py:39
  121.3 8.7 %collective-permute-start.4 = (bf16[4,128,256]{2,1,0:T(8,128)(2,1)S(1)}, bf16[4,128,256]{2,1,0:T(8,128)(2,1)S(1)}, u32[]{:S(2)}, u32[]{:S(2)}) collective-permute-start(bf16[4,128,256]{2,1,0:T(8,128)(2,1)S(1)} %copy-done.13), channel_id=1, source_target_pairs={{0,248},{8,240},{16,232},{24,224},{32,216},{40,208},{48,200},{56,1... | collective-permute-start | bytes 786440 | tf_op jit(solution)/shard_map/ppermute | solution.py:527
  129.9 6.9 %shard_map.135 = (bf16[8,2,16,2048]{3,2,1,0:T(8,128)(2,1)}, bf16[4,128,256]{2,1,0:T(8,128)(2,1)}, bf16[4,128,256]{2,1,0:T(8,128)(2,1)}) custom-call(bf16[8,2,16,2048]{3,2,1,0:T(8,128)(2,1)} %copy-done, bf16[2,4,128,256]{3,2,1,0:T(8,128)(2,1)} %get-tuple-element.75.qkv_hbm, f32[2,2,128,128]{3,2,1,0:T(8,128)} %get-tuple-element.76.soft_hbm, ...), custom_call_target="tpu_custom_call" | custom-call | flops 1073741 | bytes 12582 | tf_op jit(solution)/shard_map/pallas_call | solution.py:39
  136.8 4.8 %collective-permute-done.4.rest_3_.refs_9_ = bf16[4,128,256]{2,1,0:T(8,128)(2,1)S(1)} collective-permute-done((bf16[4,128,256]{2,1,0:T(8,128)(2,1)S(1)}, bf16[4,128,256]{2,1,0:T(8,128)(2,1)S(1)}, u32[]{:S(2)}, u32[]{:S(2)}) %collective-permute-start.4) | collective-permute-done | bytes 262176 | tf_op jit(solution)/shard_map/ppermute | solution.py:527
  142.5 24.0 %all_to_all.32.parts_ref = bf16[8,2,16,2048]{3,2,1,0:T(8,128)(2,1)} all-to-all(bf16[8,2,16,2048]{3,2,1,0:T(8,128)(2,1)} %get-tuple-element.81), channel_id=1, replica_groups=mesh['section'=32,'tp'=8] {'tp'}, dimensions={0} | all-to-all | bytes 2097152 | tf_op jit(solution)/shard_map/all_to_all | solution.py:442
  166.5 2.6 shard_map.136
  169.1 5.6 %collective-permute-start.6 = (bf16[16,2048]{1,0:T(8,128)(2,1)}, bf16[16,2048]{1,0:T(8,128)(2,1)S(1)}, u32[]{:S(2)}, u32[]{:S(2)}) collective-permute-start(bf16[16,2048]{1,0:T(8,128)(2,1)} %get-tuple-element.83), channel_id=1, source_target_pairs={{0,248},{8,0},{16,8},{24,16},{32,24},{40,32},{48,40},{56,48},{64,5... | collective-permute-start | bytes 196616 | tf_op jit(solution)/shard_map/ppermute | solution.py:512
  176.9 2.0 shard_map.137
  178.9 3.7 %all-to-all-start.4 = ((bf16[8,2,16,2048]{3,2,1,0:T(8,128)(2,1)}), bf16[8,2,16,2048]{3,2,1,0:T(8,128)(2,1)S(1)}, u32[]{:S(2)}, u32[]{:S(2)}) async-start(bf16[8,2,16,2048]{3,2,1,0:T(8,128)(2,1)} %shard_map.137), calls=%async_computation.4 | async-start | bytes 2097152 | tf_op jit(solution)/shard_map/all_to_all | solution.py:442
  182.6 5.7 %collective-permute-start.7 = (bf16[16,2048]{1,0:T(8,128)(2,1)S(1)}, bf16[16,2048]{1,0:T(8,128)(2,1)S(1)}, u32[]{:S(2)}, u32[]{:S(2)}) collective-permute-start(bf16[16,2048]{1,0:T(8,128)(2,1)S(1)} %copy-done.3), channel_id=1, source_target_pairs={{0,248},{8,240},{16,232},{24,224},{32,216},{40,208},{48,200},{56,1... | collective-permute-start | bytes 196616 | tf_op jit(solution)/shard_map/ppermute | solution.py:518
  188.3 3.2 %collective-permute-done.7.rest_0_ = bf16[16,2048]{1,0:T(8,128)(2,1)S(1)} collective-permute-done((bf16[16,2048]{1,0:T(8,128)(2,1)S(1)}, bf16[16,2048]{1,0:T(8,128)(2,1)S(1)}, u32[]{:S(2)}, u32[]{:S(2)}) %collective-permute-start.7) | collective-permute-done | bytes 65568 | tf_op jit(solution)/shard_map/ppermute | solution.py:518
  191.5 8.8 %all-to-all-done.4.g_hbm.refs_2_ = bf16[8,2,16,2048]{3,2,1,0:T(8,128)(2,1)S(1)} async-done(((bf16[8,2,16,2048]{3,2,1,0:T(8,128)(2,1)}), bf16[8,2,16,2048]{3,2,1,0:T(8,128)(2,1)S(1)}, u32[]{:S(2)}, u32[]{:S(2)}) %all-to-all-start.4) | async-done | bytes 1048608 | tf_op jit(solution)/shard_map/all_to_all | solution.py:442
  200.3 4.1 %collective-permute-start.8 = (bf16[4,128,256]{2,1,0:T(8,128)(2,1)S(1)}, bf16[4,128,256]{2,1,0:T(8,128)(2,1)S(1)}, u32[]{:S(2)}, u32[]{:S(2)}) collective-permute-start(bf16[4,128,256]{2,1,0:T(8,128)(2,1)S(1)} %copy-done.12), channel_id=1, source_target_pairs={{0,248},{8,240},{16,232},{24,224},{32,216},{40,208},{48,200},{56,1... | collective-permute-start | bytes 786440 | tf_op jit(solution)/shard_map/ppermute | solution.py:527
  204.4 8.0 %shard_map.138 = (bf16[8,3,16,2048]{3,2,1,0:T(8,128)(2,1)}, bf16[4,128,256]{2,1,0:T(8,128)(2,1)}, bf16[4,128,256]{2,1,0:T(8,128)(2,1)}) custom-call(bf16[8,2,16,2048]{3,2,1,0:T(8,128)(2,1)} %copy-done.1, bf16[2,4,128,256]{3,2,1,0:T(8,128)(2,1)} %get-tuple-element.88.qkv_hbm, f32[2,2,128,128]{3,2,1,0:T(8,128)} %get-tuple-element.89.soft_hbm, ...), custom_call_target="tpu_custom_call" | custom-call | flops 1073741 | bytes 12582 | tf_op jit(solution)/shard_map/pallas_call | solution.py:39
  213.7 7.3 %collective-permute-done.8.rest_4_.refs_10_ = bf16[4,128,256]{2,1,0:T(8,128)(2,1)S(1)} collective-permute-done((bf16[4,128,256]{2,1,0:T(8,128)(2,1)S(1)}, bf16[4,128,256]{2,1,0:T(8,128)(2,1)S(1)}, u32[]{:S(2)}, u32[]{:S(2)}) %collective-permute-start.8) | collective-permute-done | bytes 262176 | tf_op jit(solution)/shard_map/ppermute | solution.py:527
  221.1 4.3 %all-to-all-start.5 = ((bf16[8,3,16,2048]{3,2,1,0:T(8,128)(2,1)}), bf16[8,3,16,2048]{3,2,1,0:T(8,128)(2,1)}, u32[]{:S(2)}, u32[]{:S(2)}) async-start(bf16[8,3,16,2048]{3,2,1,0:T(8,128)(2,1)} %get-tuple-element.93), calls=%async_computation.5 | async-start | bytes 3145728 | tf_op jit(solution)/shard_map/all_to_all | solution.py:442
  225.4 5.9 %collective-permute-done.9.rest_5_.refs_11_ = bf16[4,128,256]{2,1,0:T(8,128)(2,1)S(1)} collective-permute-done((bf16[4,128,256]{2,1,0:T(8,128)(2,1)}, bf16[4,128,256]{2,1,0:T(8,128)(2,1)S(1)}, u32[]{:S(2)}, u32[]{:S(2)}) %collective-permute-start.9) | collective-permute-done | bytes 262176 | tf_op jit(solution)/shard_map/ppermute | solution.py:500
  232.0 8.6 %shard_map.139 = bf16[3,2048,256]{2,1,0:T(8,128)(2,1)} custom-call(bf16[8,4,16,2048]{3,2,1,0:T(8,128)(2,1)} %all_to_all.30.h_hbm.g_hbm.start.refs_0_, bf16[8,4,16,2048]{3,2,1,0:T(8,128)(2,1)} %bitcast.49, bf16[8,5,16,2048]{3,2,1,0:T(8,128)(2,1)} %bitcast.31, bf16[4,128,256]{2,1,0:T(8,128)(2,1)} %get-tuple-element.96.rest_0_.refs_6_, ...), custom_call_target="tpu_custom_call" | custom-call | flops 241591910400 | bytes 838860800 | tf_op jit(solution)/shard_map/pallas_call | solution.py:374
  240.6 6.3 %all-to-all-done.5.refs_5_.parts_ref = bf16[8,3,16,2048]{3,2,1,0:T(8,128)(2,1)} async-done(((bf16[8,3,16,2048]{3,2,1,0:T(8,128)(2,1)}), bf16[8,3,16,2048]{3,2,1,0:T(8,128)(2,1)}, u32[]{:S(2)}, u32[]{:S(2)}) %all-to-all-start.5) | async-done | bytes 1572896 | tf_op jit(solution)/shard_map/all_to_all | solution.py:442
  246.9 3.9 %shard_map.140 = bf16[256,2048]{1,0:T(8,128)(2,1)} custom-call(bf16[8,4,16,2048]{3,2,1,0:T(8,128)(2,1)} %all_to_all.30.h_hbm.g_hbm.start.refs_0_, bf16[8,2,16,2048]{3,2,1,0:T(8,128)(2,1)} %copy-done, bf16[8,2,16,2048]{3,2,1,0:T(8,128)(2,1)} %copy-done.1, bf16[8,5,16,2048]{3,2,1,0:T(8,128)(2,1)} %bitcast.32, bf16[8,5,16,2048]{3,2,1,0:T(8,128)(2,1)} %bitcast.33, ...), custom_call_target="tpu_custom_call" | custom-call | flops 805306 | bytes 5242 | tf_op jit(solution)/shard_map/pallas_call | solution.py:39
  250.8 2.7 %shard_map.141 = (bf16[16,2048]{1,0:T(8,128)(2,1)}, bf16[16,2048]{1,0:T(8,128)(2,1)}) custom-call(bf16[8,3,16,2048]{3,2,1,0:T(8,128)(2,1)} %all-to-all-done.5.refs_5_.parts_ref, bf16[3,16,2048]{2,1,0:T(8,128)(2,1)} %bitcast.47, bf16[16,2048]{1,0:T(8,128)(2,1)} %copy-done.2, bf16[2,16,2048]{2,1,0:T(8,128)(2,1)} %refs_2_.5, bf16[3,16,2048]{2,1,0:T(8,128)(2,1)} %bitcast.43, ...), custom_call_target="tpu_custom_call" | custom-call | flops 15728 | bytes 2359 | tf_op jit(solution)/shard_map/pallas_call | solution.py:39
  (47 shorter events, 9.9 us)
Async XLA Ops:
  7.2 106.2 %all-gather.5.cloned.1.call-start = ((), (), s32[]{:S(2)}) async-start(), calls=%async_computation.6 | async-start | bytes 2359296 | tf_op jit(solution)/shard_map/all_gather | solution.py:446
  10.7 31.8 %copy-start.14 = (bf16[4,16,2048]{2,1,0:T(8,128)(2,1)S(1)}, bf16[4,16,2048]{2,1,0:T(8,128)(2,1)}, u32[]{:S(2)}) copy-start(bf16[4,16,2048]{2,1,0:T(8,128)(2,1)} %get-tuple-element.62) | copy-start | bytes 786436
  42.5 22.3 %collective-permute-start = (bf16[4,16,2048]{2,1,0:T(8,128)(2,1)S(1)}, bf16[4,16,2048]{2,1,0:T(8,128)(2,1)S(1)}, u32[]{:S(2)}, u32[]{:S(2)}) collective-permute-start(bf16[4,16,2048]{2,1,0:T(8,128)(2,1)S(1)} %copy-done.14), channel_id=1, source_target_pairs={{0,248},{8,240},{16,232},{24,224},{32,216},{40,208},{48,200},{56,1... | collective-permute-start | bytes 786440 | tf_op jit(solution)/shard_map/ppermute | solution.py:480
  93.9 3.3 %collective-permute-start.1 = (bf16[16,2048]{1,0:T(8,128)(2,1)}, bf16[16,2048]{1,0:T(8,128)(2,1)S(1)}, u32[]{:S(2)}, u32[]{:S(2)}) collective-permute-start(bf16[16,2048]{1,0:T(8,128)(2,1)} %get-tuple-element.64), channel_id=1, source_target_pairs={{0,8},{8,16},{16,24},{24,32},{32,40},{40,48},{48,56},{56,64},{64,7... | collective-permute-start | bytes 196616 | tf_op jit(solution)/shard_map/ppermute | solution.py:511
  95.6 4.2 %collective-permute-start.2 = (bf16[16,2048]{1,0:T(8,128)(2,1)}, bf16[16,2048]{1,0:T(8,128)(2,1)S(1)}, u32[]{:S(2)}, u32[]{:S(2)}) collective-permute-start(bf16[16,2048]{1,0:T(8,128)(2,1)} %get-tuple-element.65), channel_id=1, source_target_pairs={{0,248},{8,0},{16,8},{24,16},{32,24},{40,32},{48,40},{56,48},{64,5... | collective-permute-start | bytes 196616 | tf_op jit(solution)/shard_map/ppermute | solution.py:512
  97.2 2.6 copy-start.5
  99.8 0.6 copy-start.7
  102.4 4.1 %copy-start.6 = (bf16[16,2048]{1,0:T(8,128)(2,1)S(1)}, bf16[16,2048]{1,0:T(8,128)(2,1)}, u32[]{:S(2)}) copy-start(bf16[16,2048]{1,0:T(8,128)(2,1)} %copy-done.5) | copy-start | bytes 196612
  102.4 18.9 %all-to-all-start.2 = ((bf16[8,2,16,2048]{3,2,1,0:T(8,128)(2,1)}), bf16[8,2,16,2048]{3,2,1,0:T(8,128)(2,1)S(1)}, u32[]{:S(2)}, u32[]{:S(2)}) async-start(bf16[8,2,16,2048]{3,2,1,0:T(8,128)(2,1)} %shard_map.133), calls=%async_computation.2 | async-start | bytes 2097152 | tf_op jit(solution)/shard_map/all_to_all | solution.py:442
  106.4 124.8 %all-gather.7.cloned.1.call-start = ((), (), s32[]{:S(2)}) async-start(), calls=%async_computation.7 | async-start | bytes 2949120 | tf_op jit(solution)/shard_map/all_gather | solution.py:446
  106.5 14.3 %collective-permute-start.3 = (bf16[16,2048]{1,0:T(8,128)(2,1)S(1)}, bf16[16,2048]{1,0:T(8,128)(2,1)S(1)}, u32[]{:S(2)}, u32[]{:S(2)}) collective-permute-start(bf16[16,2048]{1,0:T(8,128)(2,1)S(1)} %copy-done.6), channel_id=1, source_target_pairs={{0,248},{8,240},{16,232},{24,224},{32,216},{40,208},{48,200},{56,1... | collective-permute-start | bytes 196616 | tf_op jit(solution)/shard_map/ppermute | solution.py:518
  113.4 7.9 %copy-start.13 = (bf16[4,128,256]{2,1,0:T(8,128)(2,1)S(1)}, bf16[4,128,256]{2,1,0:T(8,128)(2,1)}, u32[]{:S(2)}) copy-start(bf16[4,128,256]{2,1,0:T(8,128)(2,1)} %get-tuple-element.78) | copy-start | bytes 786436
  121.3 8.7 %copy-start = (bf16[8,2,16,2048]{3,2,1,0:T(8,128)(2,1)}, bf16[8,2,16,2048]{3,2,1,0:T(8,128)(2,1)S(1)}, u32[]{:S(2)}) copy-start(bf16[8,2,16,2048]{3,2,1,0:T(8,128)(2,1)S(1)} %all-to-all-done.2.g_hbm.refs_1_) | copy-start | bytes 3145732
  121.3 20.4 %collective-permute-start.4 = (bf16[4,128,256]{2,1,0:T(8,128)(2,1)S(1)}, bf16[4,128,256]{2,1,0:T(8,128)(2,1)S(1)}, u32[]{:S(2)}, u32[]{:S(2)}) collective-permute-start(bf16[4,128,256]{2,1,0:T(8,128)(2,1)S(1)} %copy-done.13), channel_id=1, source_target_pairs={{0,248},{8,240},{16,232},{24,224},{32,216},{40,208},{48,200},{56,1... | collective-permute-start | bytes 786440 | tf_op jit(solution)/shard_map/ppermute | solution.py:527
  141.6 27.4 %copy-start.8 = (bf16[4,128,256]{2,1,0:T(8,128)(2,1)}, bf16[4,128,256]{2,1,0:T(8,128)(2,1)S(1)}, u32[]{:S(2)}) copy-start(bf16[4,128,256]{2,1,0:T(8,128)(2,1)S(1)} %collective-permute-done.4.rest_3_.refs_9_) | copy-start | bytes 786436
  169.0 31.2 %copy-start.12 = (bf16[4,128,256]{2,1,0:T(8,128)(2,1)S(1)}, bf16[4,128,256]{2,1,0:T(8,128)(2,1)}, u32[]{:S(2)}) copy-start(bf16[4,128,256]{2,1,0:T(8,128)(2,1)} %get-tuple-element.92) | copy-start | bytes 786436
  169.0 6.6 %collective-permute-start.5 = (bf16[16,2048]{1,0:T(8,128)(2,1)}, bf16[16,2048]{1,0:T(8,128)(2,1)S(1)}, u32[]{:S(2)}, u32[]{:S(2)}) collective-permute-start(bf16[16,2048]{1,0:T(8,128)(2,1)} %get-tuple-element.82), channel_id=1, source_target_pairs={{0,8},{8,16},{16,24},{24,32},{32,40},{40,48},{48,56},{56,64},{64,7... | collective-permute-start | bytes 196616 | tf_op jit(solution)/shard_map/ppermute | solution.py:511
  169.1 6.8 %collective-permute-start.6 = (bf16[16,2048]{1,0:T(8,128)(2,1)}, bf16[16,2048]{1,0:T(8,128)(2,1)S(1)}, u32[]{:S(2)}, u32[]{:S(2)}) collective-permute-start(bf16[16,2048]{1,0:T(8,128)(2,1)} %get-tuple-element.83), channel_id=1, source_target_pairs={{0,248},{8,0},{16,8},{24,16},{32,24},{40,32},{48,40},{56,48},{64,5... | collective-permute-start | bytes 196616 | tf_op jit(solution)/shard_map/ppermute | solution.py:512
  175.6 0.6 copy-start.2
  176.3 0.6 copy-start.4
  178.8 3.7 %copy-start.3 = (bf16[16,2048]{1,0:T(8,128)(2,1)S(1)}, bf16[16,2048]{1,0:T(8,128)(2,1)}, u32[]{:S(2)}) copy-start(bf16[16,2048]{1,0:T(8,128)(2,1)} %copy-done.2) | copy-start | bytes 196612
  178.9 21.4 %all-to-all-start.4 = ((bf16[8,2,16,2048]{3,2,1,0:T(8,128)(2,1)}), bf16[8,2,16,2048]{3,2,1,0:T(8,128)(2,1)S(1)}, u32[]{:S(2)}, u32[]{:S(2)}) async-start(bf16[8,2,16,2048]{3,2,1,0:T(8,128)(2,1)} %shard_map.137), calls=%async_computation.4 | async-start | bytes 2097152 | tf_op jit(solution)/shard_map/all_to_all | solution.py:442
  182.6 8.9 %collective-permute-start.7 = (bf16[16,2048]{1,0:T(8,128)(2,1)S(1)}, bf16[16,2048]{1,0:T(8,128)(2,1)S(1)}, u32[]{:S(2)}, u32[]{:S(2)}) collective-permute-start(bf16[16,2048]{1,0:T(8,128)(2,1)S(1)} %copy-done.3), channel_id=1, source_target_pairs={{0,248},{8,240},{16,232},{24,224},{32,216},{40,208},{48,200},{56,1... | collective-permute-start | bytes 196616 | tf_op jit(solution)/shard_map/ppermute | solution.py:518
  191.5 12.9 %copy-start.11 = (bf16[16,2048]{1,0:T(8,128)(2,1)}, bf16[16,2048]{1,0:T(8,128)(2,1)S(1)}, u32[]{:S(2)}) copy-start(bf16[16,2048]{1,0:T(8,128)(2,1)S(1)} %collective-permute-done.7.rest_0_) | copy-start | bytes 196612
  200.3 4.1 %copy-start.1 = (bf16[8,2,16,2048]{3,2,1,0:T(8,128)(2,1)}, bf16[8,2,16,2048]{3,2,1,0:T(8,128)(2,1)S(1)}, u32[]{:S(2)}) copy-start(bf16[8,2,16,2048]{3,2,1,0:T(8,128)(2,1)S(1)} %all-to-all-done.4.g_hbm.refs_2_) | copy-start | bytes 3145732
  200.3 20.8 %collective-permute-start.8 = (bf16[4,128,256]{2,1,0:T(8,128)(2,1)S(1)}, bf16[4,128,256]{2,1,0:T(8,128)(2,1)S(1)}, u32[]{:S(2)}, u32[]{:S(2)}) collective-permute-start(bf16[4,128,256]{2,1,0:T(8,128)(2,1)S(1)} %copy-done.12), channel_id=1, source_target_pairs={{0,248},{8,240},{16,232},{24,224},{32,216},{40,208},{48,200},{56,1... | collective-permute-start | bytes 786440 | tf_op jit(solution)/shard_map/ppermute | solution.py:527
  212.4 18.9 %collective-permute-start.9 = (bf16[4,128,256]{2,1,0:T(8,128)(2,1)}, bf16[4,128,256]{2,1,0:T(8,128)(2,1)S(1)}, u32[]{:S(2)}, u32[]{:S(2)}) collective-permute-start(bf16[4,128,256]{2,1,0:T(8,128)(2,1)} %get-tuple-element.101), channel_id=1, source_target_pairs={{0,248},{8,240},{16,232},{24,224},{32,216},{40,208},{48,200},{56,1... | collective-permute-start | bytes 786440 | tf_op jit(solution)/shard_map/ppermute | solution.py:500
  221.1 10.2 %copy-start.9 = (bf16[4,128,256]{2,1,0:T(8,128)(2,1)}, bf16[4,128,256]{2,1,0:T(8,128)(2,1)S(1)}, u32[]{:S(2)}) copy-start(bf16[4,128,256]{2,1,0:T(8,128)(2,1)S(1)} %collective-permute-done.8.rest_4_.refs_10_) | copy-start | bytes 786436
  221.1 25.8 %all-to-all-start.5 = ((bf16[8,3,16,2048]{3,2,1,0:T(8,128)(2,1)}), bf16[8,3,16,2048]{3,2,1,0:T(8,128)(2,1)}, u32[]{:S(2)}, u32[]{:S(2)}) async-start(bf16[8,3,16,2048]{3,2,1,0:T(8,128)(2,1)} %get-tuple-element.93), calls=%async_computation.5 | async-start | bytes 3145728 | tf_op jit(solution)/shard_map/all_to_all | solution.py:442
  231.2 0.7 copy-start.10
Sparse Core Ops, SparseCore 0:
  42.6 52.1 all-gather.4
  142.6 51.2 all-gather.6
